TPU v7x, 512 devices: a whole 4x4x16 slice. The times are simulated.
512 devices in a mesh: dp: 4 (over y), mp: 128 (over z, x, core).
Axes of the slice: x: 4, y: 4, z: 16, core: 2. Of those that a mesh axis runs over, the one named last changes fastest.
Arguments:
- tokens: bfloat16 [512, 8192], P(('dp', 'mp')), may hold values from -6 to 6
- counts: int32 [4], P('dp'), may hold values from 1 to 128, 320 in all
- up_blocks: bfloat16 [2048, 128, 128], P('mp'), may hold values from -0.125 to 0.125
- up_cols: int32 [128, 16], P('mp'), may hold values from 0 to 63, all different within a row
- down_blocks: bfloat16 [2048, 128, 128], P('mp'), may hold values from -0.09375 to 0.09375
- down_rows: int32 [128, 16], P('mp'), may hold values from 0 to 63, all different within a row
- cotangent: bfloat16 [512, 8192], P(('dp', 'mp')), may hold values from -6 to 6
- up_moment: bfloat16 [2048, 128, 128], P('mp'), may hold values from -1 to 1
- up_moment_scale: float32 [2048, 8], P('mp'), may hold values from 0.0005 to 0.005
- up_second: bfloat16 [2048, 128, 128], P('mp'), may hold values from 0.049804688 to 1
- up_second_scale: float32 [2048, 8], P('mp'), may hold values from 1e-06 to 1e-05
- down_moment: bfloat16 [2048, 128, 128], P('mp'), may hold values from -1 to 1
- down_moment_scale: float32 [2048, 8], P('mp'), may hold values from 0.0005 to 0.005
- down_second: bfloat16 [2048, 128, 128], P('mp'), may hold values from 0.049804688 to 1
- down_second_scale: float32 [2048, 8], P('mp'), may hold values from 1e-06 to 1e-05
Outputs:
- layer_output: bfloat16 [512, 8192], P(('dp', 'mp'))
- new_up_blocks: bfloat16 [2048, 128, 128], P('mp')
- new_up_moment: bfloat16 [2048, 128, 128], P('mp')
- new_up_moment_scale: float32 [2048, 8], P('mp')
- new_up_second: bfloat16 [2048, 128, 128], P('mp')
- new_up_second_scale: float32 [2048, 8], P('mp')
- new_down_blocks: bfloat16 [2048, 128, 128], P('mp')
- new_down_moment: bfloat16 [2048, 128, 128], P('mp')
- new_down_moment_scale: float32 [2048, 8], P('mp')
- new_down_second: bfloat16 [2048, 128, 128], P('mp')
- new_down_second_scale: float32 [2048, 8], P('mp')
Inputs may be any that keep to these rules, and one draw needn't show every extreme that they name: Each row of up_cols lists 16 different input column blocks; every column block appears somewhere. Each row of down_rows lists 16 different output row blocks; every row block appears somewhere. The first counts[r] token slots of replica r are valid; some replica is full.
All inputs are finite; a program needn't handle non-finite values. Where the computation divides by a largest or mean magnitude, that divisor is 1e-20 or more. No bound on the sum of `counts` on one device may be relied on, other than what follows from the above.
Results may differ from a plain program's by a relative error of at most 0.0057.
Values may be sent and summed in bfloat16 or wider, within the bound.
A program may use at most 64 MiB of HBM per device.

v0:
```python
import jax
import jax.numpy as jnp
from jax import lax
from jax.sharding import PartitionSpec as P

D = 8192
BLK = 128
QGROUP = 2048


beta_one = 0.9
beta_two = 0.99
learn_rate = 0.002
decay_rate = 0.1
adam_eps = 1e-08
scale_eps = 1e-06
bias_one = 1.0 - 0.9**10
bias_two = 1.0 - 0.99**10


def adam_blocks(weight, gradient, moment, moment_scale, second, second_scale):
    group_shape = (weight.shape[0], moment_scale.shape[1], QGROUP // BLK, BLK)
    grad_groups = gradient.reshape(group_shape)
    moment_old = moment.astype(jnp.float32).reshape(group_shape) * moment_scale[:, :, None, None]
    second_old = second.astype(jnp.float32).reshape(group_shape) * second_scale[:, :, None, None]
    moment_new = beta_one * moment_old + (1.0 - beta_one) * grad_groups
    second_new = beta_two * second_old + (1.0 - beta_two) * grad_groups * grad_groups
    direction = moment_new / bias_one / (jnp.sqrt(second_new / bias_two) + adam_eps)
    weight_old = weight.astype(jnp.float32).reshape(group_shape)
    weight_new = (weight_old - learn_rate * (direction + decay_rate * weight_old)).astype(
        jnp.bfloat16
    )
    moment_top = jnp.max(jnp.abs(moment_new), axis=(2, 3)) + scale_eps
    second_top = jnp.max(second_new, axis=(2, 3)) + scale_eps
    moment_code = (moment_new / moment_top[:, :, None, None]).astype(jnp.bfloat16)
    second_code = (second_new / second_top[:, :, None, None]).astype(jnp.bfloat16)
    return (
        weight_new.reshape(weight.shape),
        moment_code.reshape(weight.shape),
        moment_top,
        second_code.reshape(weight.shape),
        second_top,
    )


def per_device(
    tokens,
    counts,
    up_blocks,
    up_cols,
    down_blocks,
    down_rows,
    cotangent,
    up_moment,
    up_moment_scale,
    up_second,
    up_second_scale,
    down_moment,
    down_moment_scale,
    down_second,
    down_second_scale,
):
    local_rows = tokens.shape[0]
    col_blocks = D // BLK
    first_row = lax.axis_index("mp") * local_rows
    local_valid = (first_row + jnp.arange(local_rows, dtype=jnp.int32) < counts[0]).astype(
        jnp.bfloat16
    )[:, None]
    masked_cot = cotangent * local_valid
    col_index = up_cols[0]
    row_index = down_rows[0]
    whole_tokens, whole_cot = (
        lax.all_gather(tokens, "mp", axis=0, tiled=True),
        lax.all_gather(masked_cot, "mp", axis=0, tiled=True),
    )
    picked = jnp.take(
        whole_tokens.reshape(whole_tokens.shape[0], col_blocks, BLK), col_index, axis=1
    )
    preact = jnp.einsum("tki,koi->to", picked, up_blocks, preferred_element_type=jnp.float32)
    hidden = jax.nn.silu(preact).astype(jnp.bfloat16)
    onehot = (row_index[:, None] == jnp.arange(col_blocks, dtype=jnp.int32)[None, :]).astype(
        jnp.float32
    )
    contrib_part = jnp.einsum(
        "ti,koi->tko", hidden, down_blocks, preferred_element_type=jnp.float32
    )
    placed_part = jnp.einsum("tko,kn->tno", contrib_part, onehot, precision=lax.Precision.HIGHEST)
    summed = lax.psum_scatter(
        placed_part.reshape(lax.axis_size("mp") * local_rows, D),
        "mp",
        scatter_dimension=0,
        tiled=True,
    )
    layer_output = (summed * local_valid.astype(jnp.float32)).astype(jnp.bfloat16)
    picked_cot = jnp.take(whole_cot.reshape(whole_cot.shape[0], col_blocks, BLK), row_index, axis=1)
    hidden_grad = jnp.einsum(
        "tko,koi->ti", picked_cot, down_blocks, preferred_element_type=jnp.float32
    )
    down_grad = jnp.einsum("tko,ti->koi", picked_cot, hidden, preferred_element_type=jnp.float32)
    local_count = counts.astype(jnp.float32)
    squash = jax.nn.sigmoid(preact)
    pre_grad = (hidden_grad * squash * (1.0 + preact * (1.0 - squash))).astype(jnp.bfloat16)
    up_grad = jnp.einsum("to,tki->koi", pre_grad, picked, preferred_element_type=jnp.float32)
    up_grad, down_grad, token_total = lax.psum((up_grad, down_grad, local_count), "dp")
    up_grad = up_grad / token_total[0]
    down_grad = down_grad / token_total[0]
    up_new = adam_blocks(up_blocks, up_grad, up_moment, up_moment_scale, up_second, up_second_scale)
    down_new = adam_blocks(
        down_blocks, down_grad, down_moment, down_moment_scale, down_second, down_second_scale
    )
    return (
        layer_output,
        up_new[0],
        up_new[1],
        up_new[2],
        up_new[3],
        up_new[4],
        down_new[0],
        down_new[1],
        down_new[2],
        down_new[3],
        down_new[4],
    )


def solution(mesh):
    return jax.shard_map(
        per_device,
        mesh=mesh,
        in_specs=(
            P(("dp", "mp"), None),
            P("dp"),
            P("mp", None, None),
            P("mp", None),
            P("mp", None, None),
            P("mp", None),
            P(("dp", "mp"), None),
            P("mp", None, None),
            P("mp", None),
            P("mp", None, None),
            P("mp", None),
            P("mp", None, None),
            P("mp", None),
            P("mp", None, None),
            P("mp", None),
        ),
        out_specs=(
            P(("dp", "mp"), None),
            P("mp", None, None),
            P("mp", None, None),
            P("mp", None),
            P("mp", None, None),
            P("mp", None),
            P("mp", None, None),
            P("mp", None, None),
            P("mp", None),
            P("mp", None, None),
            P("mp", None),
        ),
        check_vma=False,
    )
```

profile of v0, /device:TPU:1, one launch (start us, length us, event | category | flops | bytes accessed | tf_op | source)
XLA Modules:
  0.0 759.4 jit_solution(6298779778628517986)
XLA Ops:
  8.6 1.4 multiply_bitcast_fusion
  12.8 146.1 %all-gather.5.cloned.1.call-done = bf16[128,1,8192]{2,1,0:T(2,128)(2,1)} async-done(((bf16[1,1,8192]{2,1,0:T(2,128)(2,1)}), bf16[128,1,8192]{2,1,0:T(2,128)(2,1)}) %all-gather.5.cloned.1.call-update) | async-done | bytes 2097168 | tf_op jit(solution)/shard_map/all_gather | solution.py:73
  158.9 8.8 %copy.129 = bf16[128,1,8192]{0,2,1:T(8,128)(2,1)S(1)} copy(bf16[128,1,8192]{2,1,0:T(2,128)(2,1)} %all-gather.5.cloned.1.call-done) | data formatting | bytes 4194304 | tf_op jit(solution)/shard_map/all_gather | solution.py:73
  167.6 2.9 copy.130
  170.6 130.0 %all-gather.7.cloned.1.call-done = bf16[128,1,8192]{2,1,0:T(2,128)(2,1)} async-done(((bf16[1,1,8192]{2,1,0:T(2,128)(2,1)}), bf16[128,1,8192]{2,1,0:T(2,128)(2,1)}) %all-gather.7.cloned.1.call-update) | async-done | bytes 2097168 | tf_op jit(solution)/shard_map/all_gather | solution.py:74
  300.5 8.8 %copy.135 = bf16[128,1,8192]{0,2,1:T(8,128)(2,1)S(1)} copy(bf16[128,1,8192]{2,1,0:T(2,128)(2,1)} %all-gather.7.cloned.1.call-done) | data formatting | bytes 4194304 | tf_op jit(solution)/shard_map/all_gather | solution.py:74
  309.3 2.9 copy.136
  312.3 2.2 gather_fusion
  314.5 2.2 gather_fusion.1
  318.5 1.6 convolution_bitcast_fusion
  320.2 9.6 %psum.22 = f32[]{:T(128)} all-reduce(f32[]{:T(128)} %bitcast.17), channel_id=1, replica_groups=mesh['dp'=4,'mp'=128] {'dp'}, use_global_device_ids=true, to_apply=%region_2.4 | all-reduce | flops 1 | bytes 8 | tf_op jit(solution)/shard_map/psum | solution.py:104
  338.0 2.1 fusion.12
  340.2 5.2 copy.164
  345.4 44.7 %all-reduce.7.cloned.1.call-done = (f32[16,128,128]{1,2,0:T(8,128)}, f32[16,128,128]{1,2,0:T(8,128)}) async-done(((f32[16,128,128]{1,2,0:T(8,128)}, f32[16,128,128]{1,2,0:T(8,128)}), (f32[16,128,128]{1,2,0:T(8,128)}, f32[16,128,128]{1,2,0:T(8,128)})) %all-reduce.7.cloned.1.call-update) | async-done | bytes 2097168 | tf_op jit(solution)/shard_map/psum | solution.py:104
  390.1 4.9 fusion.36
  397.1 4.4 divide_convert_fusion.3
  401.5 2.1 copy.147
  403.6 2.0 copy.148
  405.7 2.0 copy.150
  409.8 3.7 divide_convert_fusion.1
  413.5 2.0 copy.152
  415.5 2.0 copy.153
  418.6 332.1 %all-reduce.5.cloned.1.call-done = f32[128,8192]{1,0:T(8,128)} async-done(((f32[128,8192]{1,0:T(8,128)}), f32[128,8192]{1,0:T(8,128)}) %all-reduce.5.cloned.1.call-update) | async-done | bytes 4194320
  750.6 2.2 fusion.23
  (91 shorter events, 18.5 us)
Async XLA Ops:
  7.2 151.7 %all-gather.5.cloned.1.call-start = ((), (), s32[]{:S(2)}) async-start(), calls=%async_computation | async-start | bytes 4227072 | tf_op jit(solution)/shard_map/all_gather | solution.py:73
  7.9 292.6 %all-gather.7.cloned.1.call-start = ((), (), s32[]{:S(2)}) async-start(), calls=%async_computation.1 | async-start | bytes 4227072 | tf_op jit(solution)/shard_map/all_gather | solution.py:74
  10.1 380.1 %all-reduce.7.cloned.1.call-start = ((), (), s32[]{:S(2)}) async-start(), calls=%async_computation.3 | async-start | bytes 4194304 | tf_op jit(solution)/shard_map/psum | solution.py:104
  309.3 7.4 copy-start.6
  309.3 9.2 %copy-start = (bf16[16,128,128]{2,1,0:T(8,128)(2,1)S(1)}, bf16[16,128,128]{2,1,0:T(8,128)(2,1)}, u32[]{:S(2)}) copy-start(bf16[16,128,128]{2,1,0:T(8,128)(2,1)} %param.21) | copy-start | bytes 1572868
  317.1 14.7 %copy-start.10 = (f32[16,8]{0,1:T(8,128)S(1)}, f32[16,8]{0,1:T(8,128)}, u32[]{:S(2)}) copy-start(f32[16,8]{0,1:T(8,128)} %param.31) | copy-start | bytes 1540
  317.1 14.9 %copy-start.7 = (bf16[16,128,128]{2,1,0:T(8,128)(2,1)S(1)}, bf16[16,128,128]{2,1,0:T(8,128)(2,1)}, u32[]{:S(2)}) copy-start(bf16[16,128,128]{2,1,0:T(8,128)(2,1)} %param.30) | copy-start | bytes 1572868
  318.5 14.6 %copy-start.11 = (f32[16,8]{0,1:T(8,128)S(1)}, f32[16,8]{0,1:T(8,128)}, u32[]{:S(2)}) copy-start(f32[16,8]{0,1:T(8,128)} %param.29) | copy-start | bytes 1540
  318.5 14.8 %copy-start.8 = (bf16[16,128,128]{2,1,0:T(8,128)(2,1)S(1)}, bf16[16,128,128]{2,1,0:T(8,128)(2,1)}, u32[]{:S(2)}) copy-start(bf16[16,128,128]{2,1,0:T(8,128)(2,1)} %param.28) | copy-start | bytes 1572868
  318.5 15.1 %copy-start.12 = (f32[16,8]{0,1:T(8,128)S(1)}, f32[16,8]{0,1:T(8,128)}, u32[]{:S(2)}) copy-start(f32[16,8]{0,1:T(8,128)} %param.25) | copy-start | bytes 1540
  320.1 15.1 %copy-start.13 = (f32[16,8]{0,1:T(8,128)S(1)}, f32[16,8]{0,1:T(8,128)}, u32[]{:S(2)}) copy-start(f32[16,8]{0,1:T(8,128)} %param.27) | copy-start | bytes 1540
  320.1 430.5 %all-reduce.5.cloned.1.call-start = ((), (), s32[]{:S(2)}) async-start(), calls=%async_computation.2 | async-start | bytes 8388608
  329.7 8.3 %copy-start.14 = (s32[1,16]{1,0:T(1,128)S(1)}, s32[1,16]{1,0:T(1,128)}, u32[]{:S(2)}) copy-start(s32[1,16]{1,0:T(1,128)} %param.22) | copy-start | bytes 196
  330.7 4.7 copy-start.9
  345.4 44.7 %copy-start.4 = (bf16[16,128,128]{1,2,0:T(8,128)(2,1)S(1)}, bf16[16,128,128]{1,2,0:T(8,128)(2,1)}, u32[]{:S(2)}) copy-start(bf16[16,128,128]{1,2,0:T(8,128)(2,1)} %copy.145) | copy-start | bytes 1572868
  345.4 44.7 %copy-start.5 = (bf16[16,128,128]{1,2,0:T(8,128)(2,1)S(1)}, bf16[16,128,128]{1,2,0:T(8,128)(2,1)}, u32[]{:S(2)}) copy-start(bf16[16,128,128]{1,2,0:T(8,128)(2,1)} %copy.138) | copy-start | bytes 1572868
  390.1 7.0 copy-start.2
  397.1 12.6 %copy-start.1 = (f32[16,128,128]{1,2,0:T(8,128)S(1)}, f32[16,128,128]{1,2,0:T(8,128)}, u32[]{:S(2)}) copy-start(f32[16,128,128]{1,2,0:T(8,128)} %get-tuple-element.68) | copy-start | bytes 3145732
  401.5 8.3 %copy-start.3 = (f32[16,128,128]{1,2,0:T(8,128)S(1)}, f32[16,128,128]{1,2,0:T(8,128)}, u32[]{:S(2)}) copy-start(f32[16,128,128]{1,2,0:T(8,128)} %get-tuple-element.70) | copy-start | bytes 3145732
Sparse Core Ops, SparseCore 0:
  11.2 147.6 all-gather.4
  162.6 137.9 all-gather.6
  320.2 69.8 all-reduce.6
  393.9 356.7 all-reduce.4
where the time goes:
time: 761 us; the launch traced here: 759 us
  waiting for transfers between devices  654 us (86%)
  local copies, waits for them, and re-layouts  56 us (7%)
  other arithmetic  19.6 us (3%)
  between operations  14.7 us (2%)
  blocking collectives  9.56 us (1%)
    unnamed x5, waiting for transfers between devices  333 us
    all_gather x1, waiting for transfers between devices, per_device(): lax.all_gather(tokens, 'mp', axis=0, tiled=True)  146 us
    all_gather x1, waiting for transfers between devices, per_device(): lax.all_gather(masked_cot, 'mp', axis=0, tiled=True)  130 us
    psum x1, waiting for transfers between devices, per_device(): lax.psum((up_grad, down_grad, local_count), 'dp')  44.7 us
    unnamed x52, local copies, waits for them, and re-layouts  26.5 us
  transfers between devices with their start and end apart: 4, of which 4 were waited for; matrix products, arithmetic and copies ran while one was open for 8% of the time, Pallas kernels for 0%

commit v1 on v0

v1 whole, which is shorter than its diff:
```python
import functools

import jax
import jax.numpy as jnp
from jax import lax
from jax.experimental import pallas as pl
from jax.experimental.pallas import tpu as pltpu
from jax.sharding import PartitionSpec as P

D = 8192
BLK = 128
COLS = D // BLK
K = 16
NZ = 16
NS = 8
NY = 4
ROWS = 128
QROWS = 16
CODE_TOP = 32767.0

beta_one = 0.9
beta_two = 0.99
learn_rate = 0.002
decay_rate = 0.1
adam_eps = 1e-08
scale_eps = 1e-06
bias_one = 1.0 - 0.9**10
bias_two = 1.0 - 0.99**10

MESH = pl.DeviceIdType.MESH
F32 = jnp.float32
BF16 = jnp.bfloat16


def exchange_kernel(
    tokens_hbm,
    cot_hbm,
    counts_ref,
    cols_ref,
    rows_ref,
    up_hbm,
    down_hbm,
    layer_ref,
    grad_hbm,
    gscale_hbm,
    tokens_ref,
    cot_ref,
    up_v,
    down_v,
    zbuf,
    rowtmp,
    turned,
    idx_v,
    idx_y,
    idx_s,
    pack,
    picked,
    cbuf,
    rs_recv,
    acc,
    zsend,
    zrecv,
    gbuf,
    gscale,
    grecv,
    gscale_in,
    gsum,
    gsum_scale,
    w_sem,
    i_sem,
    o_sem,
    zs_sem,
    zr_sem,
    is_sem,
    ir_sem,
    ys_sem,
    yr_sem,
    ps_sem,
    pr_sem,
    cs_sem,
    cr_sem,
    fs_sem,
    fr_sem,
    gs_sem,
    gr_sem,
    hs_sem,
    hr_sem,
):
    y = lax.axis_index("dp")
    mp = lax.axis_index("mp")
    z = mp // NS
    s = mp % NS

    def at_z(p):
        return (y, p * NS + s)

    def at_s(p):
        return (y, z * NS + p)

    def at_y(p):
        return (p, mp)

    def off(a, d, n):
        return (a + (d % n)) % n

    def remote(src, dst, ssem, rsem, dev):
        return pltpu.make_async_remote_copy(
            src_ref=src, dst_ref=dst, send_sem=ssem, recv_sem=rsem, device_id=dev, device_id_type=MESH
        )

    barrier = pltpu.get_barrier_semaphore()
    for d in range(1, NZ):
        pl.semaphore_signal(barrier, inc=1, device_id=at_z(off(z, d, NZ)), device_id_type=MESH)
    for d in range(1, NS):
        pl.semaphore_signal(barrier, inc=1, device_id=at_s(off(s, d, NS)), device_id_type=MESH)
    for d in range(1, NY):
        pl.semaphore_signal(barrier, inc=1, device_id=at_y(off(y, d, NY)), device_id_type=MESH)

    load_up = pltpu.make_async_copy(up_hbm, up_v, w_sem.at[0])
    load_down = pltpu.make_async_copy(down_hbm, down_v, w_sem.at[1])
    load_tokens = pltpu.make_async_copy(tokens_hbm, tokens_ref, w_sem.at[2])
    load_cot = pltpu.make_async_copy(cot_hbm, cot_ref, w_sem.at[3])
    load_tokens.start()
    load_cot.start()
    load_up.start()
    load_down.start()

    valid = jnp.clip(counts_ref[0] - mp, 0, 1).astype(F32)

    load_tokens.wait()
    load_cot.wait()
    for m, ref in enumerate((tokens_ref, cot_ref)):
        for i in range(COLS):
            rowtmp[m * COLS + i : m * COLS + i + 1, :] = ref[0:1, i * BLK : (i + 1) * BLK].astype(F32)
    zbuf[z, 0:COLS, :] = rowtmp[0:COLS, :].astype(BF16)
    zbuf[z, COLS : 2 * COLS, :] = (rowtmp[COLS : 2 * COLS, :] * valid).astype(BF16)

    sub = lax.broadcasted_iota(jnp.int32, (8, BLK), 0)
    lane = lax.broadcasted_iota(jnp.int32, (8, BLK), 1)
    tile = jnp.where(sub == 2, K, 0)
    for k in range(K):
        tile = jnp.where((sub == 0) & (lane == k), cols_ref[0, k], tile)
        tile = jnp.where((sub == 1) & (lane == k), rows_ref[0, k], tile)
        tile = jnp.where((sub == 2) & (lane == rows_ref[0, k]), k, tile)
    tile = jnp.where(sub == 3, counts_ref[0], tile)
    idx_v[s] = tile
    idx_y[0] = tile
    gscale[...] = jnp.zeros_like(gscale)
    gsum_scale[...] = jnp.zeros_like(gsum_scale)
    for src in range(NS):
        rs_recv[src, K] = jnp.zeros((QROWS, BLK), BF16)

    pl.semaphore_wait(barrier, NZ + NS + NY - 3)

    def z_copy(m, w, p, o):
        part = zbuf.at[w, pl.ds(m * COLS, COLS), :]
        return remote(part, part, zs_sem.at[m, o], zr_sem.at[m, o], at_z(p))

    def z_start(m, h, e):
        z_copy(m, off(z, -h, NZ), off(z, e, NZ), (-h - e) % NZ).start()

    def z_wait(m, o):
        z_copy(m, off(z, o, NZ), off(z, 1, NZ), o).wait_recv()

    far = (8, 4, -4)
    near = ((2, 1, -1), (-2, 1, -1))

    for e in far:
        z_start(0, 0, e)
    for d in range(1, NS):
        remote(idx_v.at[s], idx_v.at[s], is_sem.at[d], ir_sem.at[d], at_s(off(s, d, NS))).start()
    for d in range(1, NY):
        remote(idx_y.at[0], idx_y.at[d], ys_sem.at[d], yr_sem.at[d], at_y(off(y, d, NY))).start()
    for e in near[0]:
        z_start(0, 0, e)
    for e in far:
        z_start(1, 0, e)
    for h in (4, -4, 8):
        z_wait(0, (-h) % NZ)
        for e in near[0]:
            z_start(0, h, e)
    for e in near[1]:
        z_start(1, 0, e)
    for h in (4, -4, 8):
        z_wait(1, (-h) % NZ)
        for e in near[1]:
            z_start(1, h, e)

    for d in range(1, NS):
        p = off(s, -d, NS)
        remote(idx_v.at[p], idx_v.at[p], is_sem.at[d], ir_sem.at[d], at_s(p)).wait_recv()
    to_smem = pltpu.make_async_copy(idx_v, idx_s, i_sem)
    to_smem.start()
    to_smem.wait()

    flat = turned.reshape(2, COLS * NZ, BLK)

    def pack_and_send(m):
        for o in range(1, NZ):
            if o % 4:
                z_wait(m, o)
        for w in range(NZ):
            flat[m, pl.ds(w, COLS, stride=NZ), :] = zbuf[w, m * COLS : (m + 1) * COLS, :].astype(F32)

        def one(i, carry):
            d = (s + i) % NS
            for k in range(K):
                pack[m, i, k] = turned[m, idx_s[d, m, k]].astype(BF16)
            remote(pack.at[m, i], picked.at[m, s], ps_sem.at[m, i], pr_sem.at[m, i], at_s(d)).start()
            return carry

        lax.fori_loop(1, NS, one, 0)
        for k in range(K):
            picked[m, s, k] = turned[m, idx_s[s, m, k]].astype(BF16)

    def wait_picked(m):
        for d in range(1, NS):
            p = off(s, -d, NS)
            remote(pack.at[m, d], picked.at[m, p], ps_sem.at[m, d], pr_sem.at[m, d], at_s(p)).wait_recv()
        return jnp.concatenate([picked[m, :, k].reshape(ROWS, BLK) for k in range(K)], axis=1)

    pack_and_send(0)
    pack_and_send(1)

    load_up.wait()
    load_down.wait()
    a_in = wait_picked(0)
    up_wide = jnp.concatenate([up_v[k] for k in range(K)], axis=1)
    preact = lax.dot_general(a_in, up_wide, (((1,), (1,)), ((), ())), preferred_element_type=F32)
    squash = 1.0 / (1.0 + jnp.exp(-preact))
    hidden = (preact * squash).astype(BF16)
    down_tall = down_v[...].reshape(K * BLK, BLK)
    contrib = lax.dot_general(hidden, down_tall, (((1,), (1,)), ((), ())), preferred_element_type=F32)
    for k in range(K):
        cbuf[:, k] = contrib[:, k * BLK : (k + 1) * BLK].astype(BF16).reshape(NS, QROWS, BLK)
    for d in range(1, NS):
        p = off(s, d, NS)
        remote(
            cbuf.at[p], rs_recv.at[s, pl.ds(0, K)], cs_sem.at[d], cr_sem.at[d], at_s(p)
        ).start()
    rs_recv[s, 0:K] = cbuf[s]

    def coded(grad):
        top = jnp.max(jnp.abs(grad), axis=0, keepdims=True)
        code = jnp.round(grad * (CODE_TOP / jnp.maximum(top, 1e-30)))
        return code.astype(jnp.int32).astype(jnp.int16), top * (1.0 / CODE_TOP)

    def grad_store(m, k, grad):
        code, scale = coded(grad)
        gbuf[m, k] = code
        gscale[m, k // 4, k % 4 : k % 4 + 1, :] = scale

    cot_in = wait_picked(1)
    down_grad = lax.dot_general(cot_in, hidden, (((0,), (0,)), ((), ())), preferred_element_type=F32)
    for k in range(K):
        grad_store(0, k, down_grad[k * BLK : (k + 1) * BLK, :])

    def grad_copies(m, d, p):
        part = (gbuf.at[m, pl.ds(p * 4, 4)], grecv.at[m, d], gs_sem.at[m, d], gr_sem.at[m, d])
        scales = (gscale.at[m, p], gscale_in.at[m, d], gs_sem.at[2 + m, d], gr_sem.at[2 + m, d])
        return remote(*part, at_y(p)), remote(*scales, at_y(p))

    def grad_start(m):
        for d in range(1, NY):
            for copy in grad_copies(m, d, off(y, d, NY)):
                copy.start()

    grad_start(0)
    hidden_grad = jnp.dot(cot_in, down_tall, preferred_element_type=F32)
    pre_grad = (hidden_grad * squash * (1.0 + preact * (1.0 - squash))).astype(BF16)
    up_grad = lax.dot_general(pre_grad, a_in, (((0,), (0,)), ((), ())), preferred_element_type=F32)
    for k in range(K):
        grad_store(1, k, up_grad[:, k * BLK : (k + 1) * BLK])
    grad_start(1)

    for d in range(1, NS):
        p = off(s, -d, NS)
        remote(
            cbuf.at[p], rs_recv.at[p, pl.ds(0, K)], cs_sem.at[d], cr_sem.at[d], at_s(p)
        ).wait_recv()

    def gather_rows(r, carry):
        total = rs_recv[0, idx_s[0, 2, r]].astype(F32)
        for src in range(1, NS):
            total = total + rs_recv[src, idx_s[src, 2, r]].astype(F32)
        acc[pl.ds(pl.multiple_of(r * NZ, NZ), NZ), :] = total
        return carry

    lax.fori_loop(0, COLS, gather_rows, 0)
    for w in range(NZ):
        zsend[w] = acc[pl.ds(w, COLS, stride=NZ), :].astype(BF16)
    for d in (8, 7, 9, 6, 10, 5, 11, 4, 12, 3, 13, 2, 14, 1, 15):
        p = off(z, d, NZ)
        remote(zsend.at[p], zrecv.at[z], fs_sem.at[d], fr_sem.at[d], at_z(p)).start()
    zrecv[z] = zsend[z]

    for d in range(1, NY):
        p = off(y, -d, NY)
        remote(idx_y.at[0], idx_y.at[d], ys_sem.at[d], yr_sem.at[d], at_y(p)).wait_recv()
    count = idx_y[0, 3:4, :]
    for d in range(1, NY):
        count = count + idx_y[d, 3:4, :]
    per_token = 1.0 / count.astype(F32)

    def sum_copies(m, q, d, p):
        part = gsum.at[m, pl.ds(q * 4, 4)]
        scales = gsum_scale.at[m, q]
        return (
            remote(part, part, hs_sem.at[m, d], hr_sem.at[m, d], at_y(p)),
            remote(scales, scales, hs_sem.at[2 + m, d], hr_sem.at[2 + m, d], at_y(p)),
        )

    for m in range(2):
        for d in range(1, NY):
            for copy in grad_copies(m, d, off(y, -d, NY)):
                copy.wait_recv()
        for b in range(4):
            own = gbuf[m, y * 4 + b].astype(F32) * gscale[m, y, b : b + 1, :]
            for d in range(1, NY):
                own = own + grecv[m, d, b].astype(F32) * gscale_in[m, d, b : b + 1, :]
            code, scale = coded(own * per_token)
            gsum[m, y * 4 + b] = code
            gsum_scale[m, y, b : b + 1, :] = scale
        for d in range(1, NY):
            for copy in sum_copies(m, y, d, off(y, d, NY)):
                copy.start()

    for d in range(1, NZ):
        p = off(z, -d, NZ)
        remote(zsend.at[p], zrecv.at[p], fs_sem.at[d], fr_sem.at[d], at_z(p)).wait_recv()
    row = zrecv[0].astype(F32)
    for w in range(1, NZ):
        row = row + zrecv[w].astype(F32)
    layer_ref[...] = row * valid

    for m in range(2):
        for d in range(1, NY):
            p = off(y, -d, NY)
            for copy in sum_copies(m, p, d, p):
                copy.wait_recv()
        pltpu.make_async_copy(gsum.at[m], grad_hbm.at[m], o_sem.at[m]).start()
    pltpu.make_async_copy(gsum_scale, gscale_hbm, o_sem.at[2]).start()

    for m in range(2):
        for o in range(1, NZ):
            z_copy(m, z, off(z, 1, NZ), o).wait_send()
        for d in range(1, NS):
            remote(pack.at[m, d], picked.at[m, s], ps_sem.at[m, d], pr_sem.at[m, d], at_s(off(s, d, NS))).wait_send()
        for d in range(1, NY):
            p = off(y, d, NY)
            for copy in grad_copies(m, d, p) + sum_copies(m, y, d, p):
                copy.wait_send()
    for d in range(1, NS):
        p = off(s, d, NS)
        remote(idx_v.at[s], idx_v.at[s], is_sem.at[d], ir_sem.at[d], at_s(p)).wait_send()
        remote(cbuf.at[p], rs_recv.at[s, pl.ds(0, K)], cs_sem.at[d], cr_sem.at[d], at_s(p)).wait_send()
    for d in range(1, NY):
        remote(idx_y.at[0], idx_y.at[d], ys_sem.at[d], yr_sem.at[d], at_y(off(y, d, NY))).wait_send()
    for d in range(1, NZ):
        p = off(z, d, NZ)
        remote(zsend.at[p], zrecv.at[z], fs_sem.at[d], fr_sem.at[d], at_z(p)).wait_send()
    for m in range(2):
        pltpu.make_async_copy(gsum.at[m], grad_hbm.at[m], o_sem.at[m]).wait()
    pltpu.make_async_copy(gsum_scale, gscale_hbm, o_sem.at[2]).wait()


def exchange(tokens, cotangent, counts, up_cols, down_rows, up_blocks, down_blocks):
    vmem = pl.BlockSpec(memory_space=pltpu.VMEM)
    smem = pl.BlockSpec(memory_space=pltpu.SMEM)
    hbm = pl.BlockSpec(memory_space=pltpu.HBM)
    dma = pltpu.SemaphoreType.DMA
    return pl.pallas_call(
        exchange_kernel,
        out_shape=(
            jax.ShapeDtypeStruct((COLS, BLK), F32),
            jax.ShapeDtypeStruct((2, K, BLK, BLK), jnp.int16),
            jax.ShapeDtypeStruct((2, NY, 8, BLK), F32),
        ),
        in_specs=[hbm, hbm, smem, smem, smem, hbm, hbm],
        out_specs=(vmem, hbm, hbm),
        scratch_shapes=[
            pltpu.VMEM((1, D), BF16),
            pltpu.VMEM((1, D), BF16),
            pltpu.VMEM((K, BLK, BLK), BF16),
            pltpu.VMEM((K, BLK, BLK), BF16),
            pltpu.VMEM((NZ, 2 * COLS, BLK), BF16),
            pltpu.VMEM((2 * COLS, BLK), F32),
            pltpu.VMEM((2, COLS, NZ, BLK), F32),
            pltpu.VMEM((NS, 8, BLK), jnp.int32),
            pltpu.VMEM((NY, 8, BLK), jnp.int32),
            pltpu.SMEM((NS, 8, BLK), jnp.int32),
            pltpu.VMEM((2, NS, K, QROWS, BLK), BF16),
            pltpu.VMEM((2, NS, K, QROWS, BLK), BF16),
            pltpu.VMEM((NS, K, QROWS, BLK), BF16),
            pltpu.VMEM((NS, K + 1, QROWS, BLK), BF16),
            pltpu.VMEM((COLS * NZ, BLK), F32),
            pltpu.VMEM((NZ, COLS, BLK), BF16),
            pltpu.VMEM((NZ, COLS, BLK), BF16),
            pltpu.VMEM((2, K, BLK, BLK), jnp.int16),
            pltpu.VMEM((2, NY, 8, BLK), F32),
            pltpu.VMEM((2, NY, 4, BLK, BLK), jnp.int16),
            pltpu.VMEM((2, NY, 8, BLK), F32),
            pltpu.VMEM((2, K, BLK, BLK), jnp.int16),
            pltpu.VMEM((2, NY, 8, BLK), F32),
            dma((4,)),
            dma,
            dma((3,)),
            dma((2, NZ)),
            dma((2, NZ)),
            dma((NS,)),
            dma((NS,)),
            dma((NY,)),
            dma((NY,)),
            dma((2, NS)),
            dma((2, NS)),
            dma((NS,)),
            dma((NS,)),
            dma((NZ,)),
            dma((NZ,)),
            dma((4, NY)),
            dma((4, NY)),
            dma((4, NY)),
            dma((4, NY)),
        ],
        compiler_params=pltpu.CompilerParams(
            collective_id=1, has_side_effects=True, vmem_limit_bytes=60 << 20
        ),
        cost_estimate=pl.CostEstimate(flops=400_000_000, bytes_accessed=4 << 20, transcendentals=16384),
        name="exchange",
    )(tokens, cotangent, counts, up_cols, down_rows, up_blocks, down_blocks)


def adam_kernel(
    row_ref,
    grad_ref,
    gscale_ref,
    um_scale,
    us_scale,
    dm_scale,
    ds_scale,
    uw_ref,
    um_ref,
    us_ref,
    dw_ref,
    dm_ref,
    ds_ref,
    layer_ref,
    nuw_ref,
    num_ref,
    nums_ref,
    nus_ref,
    nuss_ref,
    ndw_ref,
    ndm_ref,
    ndms_ref,
    nds_ref,
    ndss_ref,
):
    step = pl.program_id(0)
    per_step = uw_ref.shape[0]

    @pl.when(step == 0)
    def _():
        for i in range(COLS):
            layer_ref[0:1, i * BLK : (i + 1) * BLK] = row_ref[i : i + 1, :].astype(BF16)
        for ref in (nums_ref, nuss_ref, ndms_ref, ndss_ref):
            ref[...] = jnp.zeros_like(ref)

    lane = lax.broadcasted_iota(jnp.int32, (8, K), 1)
    groups = BLK // QROWS
    sides = (
        (0, um_scale, us_scale, uw_ref, um_ref, us_ref, nuw_ref, num_ref, nums_ref, nus_ref, nuss_ref),
        (1, dm_scale, ds_scale, dw_ref, dm_ref, ds_ref, ndw_ref, ndm_ref, ndms_ref, nds_ref, ndss_ref),
    )
    for m, m_scale, s_scale, w_ref, m_ref, s_ref, nw_ref, nm_ref, nms_ref, ns_ref, nss_ref in sides:
        for b in range(per_step):
            block = step * per_step + b
            tops_m, tops_s = [], []
            g_scale = gscale_ref[1 - m, block // 4, pl.ds(block % 4, 1), :]
            for g in range(groups):
                rows = slice(g * QROWS, (g + 1) * QROWS)
                grad = grad_ref[1 - m, b, rows, :].astype(F32) * g_scale
                m_new = (beta_one * m_scale[g, block]) * m_ref[b, rows, :].astype(F32) + (
                    1.0 - beta_one
                ) * grad
                s_new = (beta_two * s_scale[g, block]) * s_ref[b, rows, :].astype(F32) + (
                    1.0 - beta_two
                ) * (grad * grad)
                direction = (m_new * (1.0 / bias_one)) / (jnp.sqrt(s_new * (1.0 / bias_two)) + adam_eps)
                w_old = w_ref[b, rows, :].astype(F32)
                nw_ref[b, rows, :] = (w_old - learn_rate * (direction + decay_rate * w_old)).astype(BF16)
                top_m = jnp.max(jnp.abs(m_new), axis=(0, 1), keepdims=True) + scale_eps
                top_s = jnp.max(s_new, axis=(0, 1), keepdims=True) + scale_eps
                nm_ref[b, rows, :] = (m_new * (1.0 / top_m)).astype(BF16)
                ns_ref[b, rows, :] = (s_new * (1.0 / top_s)).astype(BF16)
                tops_m.append(top_m)
                tops_s.append(top_s)
            nms_ref[...] = jnp.where(lane == block, jnp.concatenate(tops_m, axis=0), nms_ref[...])
            nss_ref[...] = jnp.where(lane == block, jnp.concatenate(tops_s, axis=0), nss_ref[...])


def adam(row, grads, gscales, up, down):
    steps = 8
    per = K // steps
    whole = lambda *shape: pl.BlockSpec(shape, lambda i: (0,) * len(shape))
    smem = pl.BlockSpec(memory_space=pltpu.SMEM)
    blocks = pl.BlockSpec((per, BLK, BLK), lambda i: (i, 0, 0))
    (uw, um, ums, us, uss) = up
    (dw, dm, dms, ds, dss) = down
    big = jax.ShapeDtypeStruct((K, BLK, BLK), BF16)
    small = jax.ShapeDtypeStruct((8, K), F32)
    out = pl.pallas_call(
        adam_kernel,
        grid=(steps,),
        in_specs=[
            whole(COLS, BLK),
            pl.BlockSpec((2, per, BLK, BLK), lambda i: (0, i, 0, 0)),
            whole(2, NY, 8, BLK),
            smem,
            smem,
            smem,
            smem,
        ]
        + [blocks] * 6,
        out_specs=[whole(1, D)] + [blocks, blocks, whole(8, K), blocks, whole(8, K)] * 2,
        out_shape=[jax.ShapeDtypeStruct((1, D), BF16)] + [big, big, small, big, small] * 2,
        compiler_params=pltpu.CompilerParams(vmem_limit_bytes=60 << 20),
        cost_estimate=pl.CostEstimate(flops=20_000_000, bytes_accessed=7 << 20, transcendentals=1_000_000),
        name="adam",
    )(row, grads, gscales, ums.T, uss.T, dms.T, dss.T, uw, um, us, dw, dm, ds)
    layer = out[0]
    nuw, num, nums, nus, nuss, ndw, ndm, ndms, nds, ndss = out[1:]
    return (layer, nuw, num, nums.T, nus, nuss.T, ndw, ndm, ndms.T, nds, ndss.T)


def per_device(
    tokens,
    counts,
    up_blocks,
    up_cols,
    down_blocks,
    down_rows,
    cotangent,
    up_moment,
    up_moment_scale,
    up_second,
    up_second_scale,
    down_moment,
    down_moment_scale,
    down_second,
    down_second_scale,
):
    row, grads, gscales = exchange(tokens, cotangent, counts, up_cols, down_rows, up_blocks, down_blocks)
    return adam(
        row,
        grads,
        gscales,
        (up_blocks, up_moment, up_moment_scale, up_second, up_second_scale),
        (down_blocks, down_moment, down_moment_scale, down_second, down_second_scale),
    )


def solution(mesh):
    spread = P(("dp", "mp"), None)
    blocks = P("mp", None, None)
    table = P("mp", None)
    side = (blocks, blocks, table, blocks, table)
    return jax.shard_map(
        per_device,
        mesh=mesh,
        in_specs=(spread, P("dp"), blocks, table, blocks, table, spread)
        + (blocks, table, blocks, table) * 2,
        out_specs=(spread,) + side + side,
        check_vma=False,
    )
```

time: 761 us -> 82.4 us (0.11)
  waiting for transfers between devices: 654 us -> 0 us
  Pallas kernels: 0 us -> 80.8 us
  local copies, waits for them, and re-layouts: 56 us -> 0 us
  other arithmetic: 19.6 us -> 0 us
  between operations: 14.7 us -> 1.3 us
  blocking collectives: 9.56 us -> 0 us
    unnamed x5 -> x0, waiting for transfers between devices: 333 us -> none
    all_gather x2 -> x0, waiting for transfers between devices: 276 us -> none  [the longest x1 146 us: per_device(): lax.all_gather(tokens, 'mp', axis=0, tiled=True)]
    pallas_call x0 -> x2, Pallas kernels: none -> 80.8 us  [the longest x1 72.9 us: exchange(): pl.pallas_call(exchange_kernel, out_shape=(jax.ShapeDtypeStruct((COLS, BL...]
    psum x1 -> x0, waiting for transfers between devices: 44.7 us -> none  [per_device(): lax.psum((up_grad, down_grad, local_count), 'dp')]
    unnamed x52 -> x0, local copies, waits for them, and re-layouts: 26.5 us -> none
    all_gather x2 -> x0, local copies, waits for them, and re-layouts: 17.5 us -> none  [the longest x1 8.77 us: per_device(): lax.all_gather(masked_cot, 'mp', axis=0, tiled=True)]
    convert_element_type x3 -> x0, other arithmetic: 10.3 us -> none  [the longest x2 8.06 us: adam_blocks(): (moment_new / moment_top[:, :, None, None]).astype(jnp.bfloat16)]
    psum x1 -> x0, blocking collectives: 9.56 us -> none  [per_device(): lax.psum((up_grad, down_grad, local_count), 'dp')]
  transfers between devices with their start and end apart: 4 -> 0, of which waited for: 4 -> 0; matrix products, arithmetic and copies ran while one was open for 8% -> 0% of each run, Pallas kernels for 0% -> 0%
where the time goes in v1:
time: 82.4 us; the launch traced here: 82.1 us
  Pallas kernels  80.8 us (98%)
  between operations  1.3 us (2%)
    pallas_call x1, Pallas kernels, exchange(): pl.pallas_call(exchange_kernel, out_shape=(jax.ShapeDtypeStruct((COLS, BL...  72.9 us
    pallas_call x1, Pallas kernels, adam(): pl.pallas_call(adam_kernel, grid=(steps,), in_specs=[whole(COLS, BLK), pl...  7.89 us

profile of v1, /device:TPU:1, one launch (start us, length us, event | category | flops | bytes accessed | tf_op | source)
XLA Modules:
  0.0 82.1 jit_solution(5895834665606970543)
XLA Ops:
  1.3 72.9 %exchange.1 = (f32[64,128]{1,0:T(8,128)}, s16[2,16,128,128]{3,2,1,0:T(8,128)(2,1)}, f32[2,4,8,128]{3,2,1,0:T(8,128)}) custom-call(bf16[1,8192]{1,0:T(2,128)(2,1)} %tokens_hbm.1, bf16[1,8192]{1,0:T(2,128)(2,1)} %cot_hbm.1, s32[1]{0:T(128)S(6)} %copy.26.counts_ref, s32[1,16]{1,0:T(1,128)} %cols_ref.1, s32[1,16]{1,0:T(1,128)} %rows_ref.1, ...), custom_call_target="tpu_custom_call" | custom-call | flops 400000000 | bytes 4194304 | tf_op jit(solution)/shard_map/exchange/pallas_call | solution.py:372
  74.2 7.9 %adam.1 = (bf16[1,8192]{1,0:T(2,128)(2,1)}, bf16[16,128,128]{2,1,0:T(8,128)(2,1)}, bf16[16,128,128]{2,1,0:T(8,128)(2,1)}, f32[8,16]{1,0:T(8,128)}, bf16[16,128,1...) custom-call(f32[64,128]{1,0:T(8,128)} %get-tuple-element.25.row_ref,, ...), custom_call_target="tpu_custom_call" | custom-call | flops 20000000 | bytes 7340032 | tf_op jit(solution)/shard_map/adam/pallas_call | solution.py:512

commit v2 on v1

v2 whole, which is shorter than its diff:
```python
import functools

import jax
import jax.numpy as jnp
from jax import lax
from jax.experimental import pallas as pl
from jax.experimental.pallas import tpu as pltpu
from jax.sharding import PartitionSpec as P

D = 8192
BLK = 128
COLS = D // BLK
K = 16
NZ = 16
NS = 8
NY = 4
ROWS = 128
QROWS = 16
GROUPS = 8
CODE_TOP = 32767.0
Z_PEERS = (8, 4, -4, 2, -2, 1, -1)

beta_one = 0.9
beta_two = 0.99
learn_rate = 0.002
decay_rate = 0.1
adam_eps = 1e-08
scale_eps = 1e-06
bias_one = 1.0 - 0.9**10
bias_two = 1.0 - 0.99**10

MESH = pl.DeviceIdType.MESH
F32 = jnp.float32
BF16 = jnp.bfloat16


def exchange_kernel(*refs):
    (tokens_hbm, cot_hbm, counts_hbm, cols_hbm, rows_hbm) = refs[:5]
    states_hbm = (refs[5:8], refs[8:11])
    scales_hbm = refs[11:15]
    layer_hbm = refs[15]
    new_hbm = (refs[16:19], refs[19:22])
    new_scales_hbm = refs[22:26]
    (
        tokens_ref,
        cot_ref,
        counts_ref,
        cols_ref,
        rows_ref,
        layer_ref,
        states_v,
        scales_s,
        scales_v,
        zbuf,
        rowtmp,
        turned,
        idx_v,
        idx_y,
        idx_s,
        pack,
        picked,
        cbuf,
        rs_recv,
        acc,
        zsend,
        hub_in,
        hub_out,
        zrecv,
        gbuf,
        gscale,
        relay,
        rscale,
        grecv,
        gscale_in,
        gsum,
        gsum_scale,
        w_sem,
        i_sem,
        o_sem,
        zs_sem,
        zr_sem,
        is_sem,
        ir_sem,
        ys_sem,
        yr_sem,
        ps_sem,
        pr_sem,
        cs_sem,
        cr_sem,
        fs_sem,
        fr_sem,
        gs_sem,
        gr_sem,
    ) = refs[26:]
    y = lax.axis_index("dp")
    mp = lax.axis_index("mp")
    z = mp // NS
    s = mp % NS

    def at_z(p):
        return (y, p * NS + s)

    def at_s(p):
        return (y, z * NS + p)

    def at_y(p):
        return (p, mp)

    def off(a, d, n):
        return (a + (d % n)) % n

    def remote(src, dst, ssem, rsem, dev):
        return pltpu.make_async_remote_copy(
            src_ref=src, dst_ref=dst, send_sem=ssem, recv_sem=rsem, device_id=dev, device_id_type=MESH
        )

    barrier = pltpu.get_barrier_semaphore()
    for d in Z_PEERS:
        pl.semaphore_signal(barrier, inc=1, device_id=at_z(off(z, d, NZ)), device_id_type=MESH)
    for d in range(1, NS):
        pl.semaphore_signal(barrier, inc=1, device_id=at_s(off(s, d, NS)), device_id_type=MESH)
    for d in range(1, NY):
        pl.semaphore_signal(barrier, inc=1, device_id=at_y(off(y, d, NY)), device_id_type=MESH)

    loads = [
        pltpu.make_async_copy(src, dst, w_sem.at[i])
        for i, (src, dst) in enumerate(
            (
                (counts_hbm, counts_ref),
                (cols_hbm, cols_ref),
                (rows_hbm, rows_ref),
                (tokens_hbm, tokens_ref),
                (cot_hbm, cot_ref),
            )
        )
    ]
    state_loads = [
        [pltpu.make_async_copy(states_hbm[m][i], states_v.at[m, i], w_sem.at[5 + 3 * m + i]) for i in range(3)]
        for m in range(2)
    ]
    scale_loads = [pltpu.make_async_copy(scales_hbm[i], scales_s.at[i], w_sem.at[11 + i]) for i in range(4)]
    for copy in loads:
        copy.start()
    state_loads[1][0].start()
    state_loads[0][0].start()
    for copy in loads[:3]:
        copy.wait()

    valid = jnp.clip(counts_ref[0] - mp, 0, 1).astype(F32)

    sub = lax.broadcasted_iota(jnp.int32, (8, BLK), 0)
    lane = lax.broadcasted_iota(jnp.int32, (8, BLK), 1)
    tile = jnp.where(sub == 2, K, 0)
    for k in range(K):
        tile = jnp.where((sub == 0) & (lane == k), cols_ref[0, k], tile)
        tile = jnp.where((sub == 1) & (lane == k), rows_ref[0, k], tile)
        tile = jnp.where((sub == 2) & (lane == rows_ref[0, k]), k, tile)
    tile = jnp.where(sub == 3, counts_ref[0], tile)
    idx_v[s] = tile
    idx_y[0] = tile
    loads[3].wait()
    loads[4].wait()
    for m, ref in enumerate((tokens_ref, cot_ref)):
        for i in range(COLS):
            rowtmp[m * COLS + i : m * COLS + i + 1, :] = ref[0:1, i * BLK : (i + 1) * BLK].astype(F32)
    zbuf[z, 0:COLS, :] = rowtmp[0:COLS, :].astype(BF16)
    zbuf[z, COLS : 2 * COLS, :] = (rowtmp[COLS : 2 * COLS, :] * valid).astype(BF16)

    pl.semaphore_wait(barrier, len(Z_PEERS) + NS + NY - 2)

    def z_copy(m, w, p, o):
        part = zbuf.at[w, pl.ds(m * COLS, COLS), :]
        return remote(part, part, zs_sem.at[m, o], zr_sem.at[m, o], at_z(p))

    def z_start(m, h, e):
        z_copy(m, off(z, -h, NZ), off(z, e, NZ), (-h - e) % NZ).start()

    def z_wait(m, o):
        z_copy(m, off(z, o, NZ), off(z, 1, NZ), o).wait_recv()

    far = (8, 4, -4)
    near = ((2, 1, -1), (-2, 1, -1))

    for e in far:
        z_start(0, 0, e)
    for d in range(1, NS):
        remote(idx_v.at[s], idx_v.at[s], is_sem.at[d], ir_sem.at[d], at_s(off(s, d, NS))).start()
    for d in range(1, NY):
        remote(idx_y.at[0], idx_y.at[d], ys_sem.at[d], yr_sem.at[d], at_y(off(y, d, NY))).start()
    for e in near[0]:
        z_start(0, 0, e)
    for e in far:
        z_start(1, 0, e)
    for m in range(2):
        state_loads[m][1].start()
        state_loads[m][2].start()
    for copy in scale_loads:
        copy.start()
    for ref in (gscale, rscale, gsum_scale, scales_v):
        ref[...] = jnp.zeros_like(ref)
    for src in range(NS):
        rs_recv[src, K] = jnp.zeros((QROWS, BLK), BF16)

    for d in range(1, NS):
        p = off(s, -d, NS)
        remote(idx_v.at[p], idx_v.at[p], is_sem.at[d], ir_sem.at[d], at_s(p)).wait_recv()
    to_smem = pltpu.make_async_copy(idx_v, idx_s, i_sem)
    to_smem.start()

    for h in (4, -4, 8):
        z_wait(0, (-h) % NZ)
        for e in near[0]:
            z_start(0, h, e)
    for e in near[1]:
        z_start(1, 0, e)
    for h in (4, -4, 8):
        z_wait(1, (-h) % NZ)
        for e in near[1]:
            z_start(1, h, e)

    flat = turned.reshape(2, COLS * NZ, BLK)

    to_smem.wait()

    def pack_and_send(m):
        for o in range(1, NZ):
            if o % 4:
                z_wait(m, o)
        for w in range(NZ):
            flat[m, pl.ds(w, COLS, stride=NZ), :] = zbuf[w, m * COLS : (m + 1) * COLS, :].astype(F32)

        def one(i, carry):
            d = (s + i) % NS
            for k in range(K):
                pack[m, i, k] = turned[m, idx_s[d, m, k]].astype(BF16)
            remote(pack.at[m, i], picked.at[m, s], ps_sem.at[m, i], pr_sem.at[m, i], at_s(d)).start()
            return carry

        lax.fori_loop(1, NS, one, 0)
        for k in range(K):
            picked[m, s, k] = turned[m, idx_s[s, m, k]].astype(BF16)

    def wait_picked(m):
        for d in range(1, NS):
            p = off(s, -d, NS)
            remote(pack.at[m, d], picked.at[m, p], ps_sem.at[m, d], pr_sem.at[m, d], at_s(p)).wait_recv()
        return jnp.concatenate([picked[m, :, k].reshape(ROWS, BLK) for k in range(K)], axis=1)

    pack_and_send(0)
    pack_and_send(1)

    state_loads[1][0].wait()
    state_loads[0][0].wait()
    a_in = wait_picked(0)
    up_wide = jnp.concatenate([states_v[1, 0, k] for k in range(K)], axis=1)
    preact = lax.dot_general(a_in, up_wide, (((1,), (1,)), ((), ())), preferred_element_type=F32)
    squash = 1.0 / (1.0 + jnp.exp(-preact))
    hidden = (preact * squash).astype(BF16)
    down_tall = states_v[0, 0].reshape(K * BLK, BLK)
    contrib = lax.dot_general(hidden, down_tall, (((1,), (1,)), ((), ())), preferred_element_type=F32)
    for k in range(K):
        cbuf[:, k] = contrib[:, k * BLK : (k + 1) * BLK].astype(BF16).reshape(NS, QROWS, BLK)
    for d in range(1, NS):
        p = off(s, d, NS)
        remote(
            cbuf.at[p], rs_recv.at[s, pl.ds(0, K)], cs_sem.at[d], cr_sem.at[d], at_s(p)
        ).start()
    rs_recv[s, 0:K] = cbuf[s]

    def coded(grad):
        top = jnp.max(jnp.abs(grad), axis=0, keepdims=True)
        code = jnp.round(grad * (CODE_TOP / jnp.maximum(top, 1e-30)))
        return code.astype(jnp.int32).astype(jnp.int16), top * (1.0 / CODE_TOP)

    def grad_store(m, k, grad):
        code, scale = coded(grad)
        gbuf[m, k // 4, k // 2 % 2, k % 2] = code
        gscale[m, k // 4, k // 2 % 2, k % 2 : k % 2 + 1, :] = scale

    def pair(msg, m, buf, scl, at_src, to, to_scl, at_dst, p):
        return (
            remote(buf.at[at_src], to.at[at_dst], gs_sem.at[m, msg], gr_sem.at[m, msg], at_y(p)),
            remote(scl.at[at_src], to_scl.at[at_dst], gs_sem.at[m, 10 + msg], gr_sem.at[m, 10 + msg], at_y(p)),
        )

    left, right, across = off(y, -1, NY), off(y, 1, NY), off(y, 2, NY)

    def grad_msg(m, msg):
        raw, done = (m, gbuf, gscale), (m, gsum, gsum_scale)
        if msg == 0:
            return pair(msg, *raw, (m, across, 1), grecv, gscale_in, (m, 0), right)
        if msg == 1:
            return pair(msg, *raw, (m, across, 0), grecv, gscale_in, (m, 1), left)
        if msg == 2:
            return pair(msg, *raw, (m, right, 0), grecv, gscale_in, (m, 2), right)
        if msg == 3:
            return pair(msg, *raw, (m, left, 1), grecv, gscale_in, (m, 3), left)
        if msg == 4:
            return pair(msg, m, relay, rscale, (m, 1), grecv, gscale_in, (m, 4), right)
        if msg == 5:
            return pair(msg, m, relay, rscale, (m, 0), grecv, gscale_in, (m, 5), left)
        if msg == 6:
            return pair(msg, *done, (m, y), gsum, gsum_scale, (m, y), right)
        if msg == 7:
            return pair(msg, *done, (m, y), gsum, gsum_scale, (m, y), left)
        if msg == 8:
            return pair(msg, *done, (m, left, 1), gsum, gsum_scale, (m, left, 1), right)
        return pair(msg, *done, (m, right, 0), gsum, gsum_scale, (m, right, 0), left)

    def grad_send(m, *msgs):
        for msg in msgs:
            for copy in grad_msg(m, msg):
                copy.start()

    def grad_sent(m, *msgs):
        for msg in msgs:
            for copy in grad_msg(m, msg):
                copy.wait_send()

    def grad_wait(m, msg):
        for copy in grad_msg(m, msg):
            copy.wait_recv()

    def grad_back(m, msg, q):
        at = (m, q) if msg < 8 else (m, q, 9 - msg)
        for copy in pair(msg, m, gsum, gsum_scale, at, gsum, gsum_scale, at, left):
            copy.wait_recv()

    def value(buf, scl, at, b):
        return buf[(*at, b)].astype(F32) * scl[(*at, slice(b, b + 1), slice(None))]

    def pass_sum(m, msg, half, q, out):
        grad_wait(m, msg)
        for b in range(2):
            code, scale = coded(value(grecv, gscale_in, (m, msg), b) + value(gbuf, gscale, (m, q, half), b))
            relay[m, half, b] = code
            rscale[m, half, b : b + 1, :] = scale
        grad_send(m, out)

    def own_sum(m, half, msgs):
        for msg in msgs:
            grad_wait(m, msg)
        for b in range(2):
            total = value(gbuf, gscale, (m, y, half), b)
            for msg in msgs:
                total = total + value(grecv, gscale_in, (m, msg), b)
            code, scale = coded(total * per_token)
            gsum[m, y, half, b] = code
            gsum_scale[m, y, half, b : b + 1, :] = scale

    lane = lax.broadcasted_iota(jnp.int32, (8, K), 1)

    def adam(m, q):
        def block_step(i, carry):
            half, b = i // 2, i % 2
            block = q * 4 + i
            g_scale = gsum_scale[m, q, half, pl.ds(b, 1), :]
            moments, seconds = [], []
            for g in range(GROUPS):
                rows = slice(g * QROWS, (g + 1) * QROWS)
                grad = gsum[m, q, half, b, rows, :].astype(F32) * g_scale
                m_scale = beta_one * scales_s[2 * m, g, block]
                s_scale = beta_two * scales_s[2 * m + 1, g, block]
                m_new = m_scale * states_v[m, 1, block, rows, :].astype(F32) + (1.0 - beta_one) * grad
                s_new = s_scale * states_v[m, 2, block, rows, :].astype(F32) + (1.0 - beta_two) * (grad * grad)
                second = s_new * (1.0 / bias_two)
                root = second * lax.rsqrt(second) + adam_eps
                w_old = states_v[m, 0, block, rows, :].astype(F32)
                w_new = w_old * (1.0 - learn_rate * decay_rate) - (m_new * (learn_rate / bias_one)) * pl.reciprocal(
                    root, approx=True
                )
                states_v[m, 0, block, rows, :] = w_new.astype(BF16)
                moments.append(m_new)
                seconds.append(s_new)
            for j, values in ((0, moments), (1, seconds)):
                tops = jnp.concatenate([jnp.max(jnp.abs(v), axis=0, keepdims=True) for v in values], axis=0)
                top = jnp.max(tops, axis=1, keepdims=True) + scale_eps
                inverse = jnp.broadcast_to(1.0 / top, (8, BLK))
                for g in range(GROUPS):
                    rows = slice(g * QROWS, (g + 1) * QROWS)
                    states_v[m, 1 + j, block, rows, :] = (values[g] * inverse[g : g + 1, :]).astype(BF16)
                scales_v[2 * m + j] = jnp.where(lane == block, top, scales_v[2 * m + j])
            return carry

        lax.fori_loop(0, 4, block_step, 0)
        for i in range(3):
            out_copy(m, q, i).start()

    def out_copy(m, q, i):
        rows = pl.ds(q * 4, 4)
        return pltpu.make_async_copy(states_v.at[m, i, rows], new_hbm[m][i].at[rows], o_sem.at[m, i, q])

    cot_in = wait_picked(1)
    down_grad = lax.dot_general(cot_in, hidden, (((0,), (0,)), ((), ())), preferred_element_type=F32)
    for k in range(K):
        grad_store(0, k, down_grad[k * BLK : (k + 1) * BLK, :])

    grad_send(0, 0, 1, 2, 3)
    hidden_grad = jnp.dot(cot_in, down_tall, preferred_element_type=F32)
    pre_grad = (hidden_grad * squash * (1.0 + preact * (1.0 - squash))).astype(BF16)
    up_grad = lax.dot_general(pre_grad, a_in, (((0,), (0,)), ((), ())), preferred_element_type=F32)
    for k in range(K):
        grad_store(1, k, up_grad[:, k * BLK : (k + 1) * BLK])
    grad_send(1, 0, 1, 2, 3)

    for m in range(2):
        for o in range(1, NZ):
            z_copy(m, z, off(z, 1, NZ), o).wait_send()
        for d in range(1, NS):
            remote(pack.at[m, d], picked.at[m, s], ps_sem.at[m, d], pr_sem.at[m, d], at_s(off(s, d, NS))).wait_send()
    for d in range(1, NS):
        remote(idx_v.at[s], idx_v.at[s], is_sem.at[d], ir_sem.at[d], at_s(off(s, d, NS))).wait_send()
    for d in range(1, NY):
        remote(idx_y.at[0], idx_y.at[d], ys_sem.at[d], yr_sem.at[d], at_y(off(y, d, NY))).wait_send()
    for d in range(1, NY):
        p = off(y, -d, NY)
        remote(idx_y.at[0], idx_y.at[d], ys_sem.at[d], yr_sem.at[d], at_y(p)).wait_recv()
    count = idx_y[0, 3:4, :]
    for d in range(1, NY):
        count = count + idx_y[d, 3:4, :]
    per_token = 1.0 / count.astype(F32)

    pass_sum(0, 0, 1, right, 4)
    pass_sum(0, 1, 0, left, 5)

    for d in range(1, NS):
        p = off(s, -d, NS)
        remote(
            cbuf.at[p], rs_recv.at[p, pl.ds(0, K)], cs_sem.at[d], cr_sem.at[d], at_s(p)
        ).wait_recv()

    def gather_rows(r, carry):
        total = rs_recv[0, idx_s[0, 2, r]].astype(F32)
        for src in range(1, NS):
            total = total + rs_recv[src, idx_s[src, 2, r]].astype(F32)
        acc[pl.ds(pl.multiple_of(r * NZ, NZ), NZ), :] = total
        return carry

    lax.fori_loop(0, COLS, gather_rows, 0)
    for w in range(NZ):
        zsend[w % 4, w // 4] = acc[pl.ds(w, COLS, stride=NZ), :].astype(BF16)

    core = s % 2
    hubs = (off(z + 12 * core, 2, NZ), off(z, 1, NZ), off(z, -1, NZ))
    hub_from = (off(z + 4 * core, -2, NZ), off(z, -1, NZ), off(z, 1, NZ))

    def hub_copy(j, p):
        return remote(zsend.at[p % 4], hub_in.at[j], fs_sem.at[j], fr_sem.at[j], at_z(p))

    def row_copy(j, p):
        return remote(hub_out.at[p // 4], zrecv.at[j], fs_sem.at[4 + j], fr_sem.at[4 + j], at_z(p))

    for j in range(3):
        hub_copy(j, hubs[j]).start()

    pass_sum(1, 0, 1, right, 4)
    pass_sum(1, 1, 0, left, 5)
    own_sum(0, 0, (2, 5))
    own_sum(0, 1, (3, 4))
    grad_send(0, 6, 7)

    for j in range(3):
        hub_copy(j, hub_from[j]).wait_recv()
    for w in range(4):
        part = zsend[z % 4, w].astype(F32)
        for j in range(3):
            part = part + hub_in[j, w].astype(F32)
        hub_out[w] = part.astype(BF16)
    for j in (2, 1, 3):
        row_copy(j, off(z, 4 * j, NZ)).start()

    own_sum(1, 0, (2, 5))
    own_sum(1, 1, (3, 4))
    grad_send(1, 6, 7)
    for m in range(2):
        for i in (1, 2):
            state_loads[m][i].wait()
    for copy in scale_loads:
        copy.wait()
    adam(0, y)
    adam(1, y)
    grad_back(0, 6, left)
    grad_send(0, 8)
    grad_back(0, 7, right)
    grad_send(0, 9)

    grad_back(1, 6, left)
    grad_send(1, 8)
    grad_back(1, 7, right)
    grad_send(1, 9)
    adam(0, left)
    adam(0, right)
    for j in (1, 2, 3):
        row_copy(j, off(z, -4 * j, NZ)).wait_recv()
    row = hub_out[z // 4].astype(F32)
    for j in (1, 2, 3):
        row = row + zrecv[j].astype(F32)
    row = row * valid
    for i in range(COLS):
        layer_ref[0:1, i * BLK : (i + 1) * BLK] = row[i : i + 1, :].astype(BF16)
    layer_out = pltpu.make_async_copy(layer_ref, layer_hbm, w_sem.at[0])
    layer_out.start()
    for j in range(3):
        hub_copy(j, hubs[j]).wait_send()
    for j in (1, 2, 3):
        row_copy(j, off(z, 4 * j, NZ)).wait_send()
    for d in range(1, NS):
        p = off(s, d, NS)
        remote(cbuf.at[p], rs_recv.at[s, pl.ds(0, K)], cs_sem.at[d], cr_sem.at[d], at_s(p)).wait_send()
    for m in range(2):
        grad_sent(m, 0, 1, 2, 3, 4, 5)
    adam(1, left)
    adam(1, right)
    for m in range(2):
        grad_back(m, 8, across)
        grad_back(m, 9, across)
        adam(m, across)
    scale_out = [pltpu.make_async_copy(scales_v.at[i], new_scales_hbm[i], w_sem.at[1 + i]) for i in range(4)]
    for copy in scale_out:
        copy.start()
    for m in range(2):
        grad_sent(m, 6, 7, 8, 9)
    layer_out.wait()
    for m in range(2):
        for q in range(NY):
            for i in range(3):
                out_copy(m, q, i).wait()
    for copy in scale_out:
        copy.wait()


def deliver_kernel(*refs):
    n = 11
    held, in_sem, out_sem = refs[2 * n : 3 * n], refs[3 * n], refs[3 * n + 1]
    parts = []
    for i in range(n):
        if len(refs[i].shape) == 3:
            parts += [(i, pl.ds(0, K // 2)), (i, pl.ds(K // 2, K // 2))]
        else:
            parts.append((i, pl.ds(0, refs[i].shape[0])))
    loads = [pltpu.make_async_copy(refs[i].at[at], held[i].at[at], in_sem.at[j]) for j, (i, at) in enumerate(parts)]
    stores = [
        pltpu.make_async_copy(held[i].at[at], refs[n + i].at[at], out_sem.at[j]) for j, (i, at) in enumerate(parts)
    ]
    for load in loads:
        load.start()
    for load, store in zip(loads, stores):
        load.wait()
        store.start()
    for store in stores:
        store.wait()


def exchange(tokens, cotangent, counts, up_cols, down_rows, up, down):
    hbm = pl.BlockSpec(memory_space=pltpu.HBM)
    free = pl.BlockSpec(memory_space=pl.ANY)
    dma = pltpu.SemaphoreType.DMA
    (uw, um, ums, us, uss) = up
    (dw, dm, dms, ds, dss) = down
    big = jax.ShapeDtypeStruct((K, BLK, BLK), BF16)
    small = jax.ShapeDtypeStruct((GROUPS, K), F32)
    shapes = (jax.ShapeDtypeStruct((1, D), BF16),) + (big,) * 6 + (small,) * 4
    results = pl.pallas_call(
        exchange_kernel,
        out_shape=shapes,
        in_specs=[hbm] * 15,
        out_specs=(free,) * 11,
        scratch_shapes=[
            pltpu.VMEM((1, D), BF16),
            pltpu.VMEM((1, D), BF16),
            pltpu.SMEM((1,), jnp.int32),
            pltpu.SMEM((1, K), jnp.int32),
            pltpu.SMEM((1, K), jnp.int32),
            pltpu.VMEM((1, D), BF16),
            pltpu.VMEM((2, 3, K, BLK, BLK), BF16),
            pltpu.SMEM((4, GROUPS, K), F32),
            pltpu.VMEM((4, GROUPS, K), F32),
            pltpu.VMEM((NZ, 2 * COLS, BLK), BF16),
            pltpu.VMEM((2 * COLS, BLK), F32),
            pltpu.VMEM((2, COLS, NZ, BLK), F32),
            pltpu.VMEM((NS, 8, BLK), jnp.int32),
            pltpu.VMEM((NY, 8, BLK), jnp.int32),
            pltpu.SMEM((NS, 8, BLK), jnp.int32),
            pltpu.VMEM((2, NS, K, QROWS, BLK), BF16),
            pltpu.VMEM((2, NS, K, QROWS, BLK), BF16),
            pltpu.VMEM((NS, K, QROWS, BLK), BF16),
            pltpu.VMEM((NS, K + 1, QROWS, BLK), BF16),
            pltpu.VMEM((COLS * NZ, BLK), F32),
            pltpu.VMEM((4, 4, COLS, BLK), BF16),
            pltpu.VMEM((3, 4, COLS, BLK), BF16),
            pltpu.VMEM((4, COLS, BLK), BF16),
            pltpu.VMEM((4, COLS, BLK), BF16),
            pltpu.VMEM((2, NY, 2, 2, BLK, BLK), jnp.int16),
            pltpu.VMEM((2, NY, 2, 8, BLK), F32),
            pltpu.VMEM((2, 2, 2, BLK, BLK), jnp.int16),
            pltpu.VMEM((2, 2, 8, BLK), F32),
            pltpu.VMEM((2, 6, 2, BLK, BLK), jnp.int16),
            pltpu.VMEM((2, 6, 8, BLK), F32),
            pltpu.VMEM((2, NY, 2, 2, BLK, BLK), jnp.int16),
            pltpu.VMEM((2, NY, 2, 8, BLK), F32),
            dma((15,)),
            dma,
            dma((2, 3, NY)),
            dma((2, NZ)),
            dma((2, NZ)),
            dma((NS,)),
            dma((NS,)),
            dma((NY,)),
            dma((NY,)),
            dma((2, NS)),
            dma((2, NS)),
            dma((NS,)),
            dma((NS,)),
            dma((8,)),
            dma((8,)),
            dma((2, 20)),
            dma((2, 20)),
        ],
        compiler_params=pltpu.CompilerParams(
            collective_id=1, has_side_effects=True, vmem_limit_bytes=60 << 20
        ),
        cost_estimate=pl.CostEstimate(flops=400_000_000, bytes_accessed=8 << 20, transcendentals=1_000_000),
        name="exchange",
    )(
        tokens,
        cotangent,
        counts,
        up_cols,
        down_rows,
        dw,
        dm,
        ds,
        uw,
        um,
        us,
        dms.T,
        dss.T,
        ums.T,
        uss.T,
    )
    results = pl.pallas_call(
        deliver_kernel,
        out_shape=shapes,
        in_specs=[free] * 11,
        out_specs=(hbm,) * 11,
        scratch_shapes=[pltpu.VMEM(a.shape, a.dtype) for a in shapes] + [dma((17,)), dma((17,))],
        compiler_params=pltpu.CompilerParams(vmem_limit_bytes=60 << 20),
        name="deliver",
    )(*results)
    (layer, ndw, ndm, nds, nuw, num, nus, ndms, ndss, nums, nuss) = results
    return (layer, nuw, num, nums.T, nus, nuss.T, ndw, ndm, ndms.T, nds, ndss.T)


def per_device(
    tokens,
    counts,
    up_blocks,
    up_cols,
    down_blocks,
    down_rows,
    cotangent,
    up_moment,
    up_moment_scale,
    up_second,
    up_second_scale,
    down_moment,
    down_moment_scale,
    down_second,
    down_second_scale,
):
    return exchange(
        tokens,
        cotangent,
        counts,
        up_cols,
        down_rows,
        (up_blocks, up_moment, up_moment_scale, up_second, up_second_scale),
        (down_blocks, down_moment, down_moment_scale, down_second, down_second_scale),
    )


def solution(mesh):
    spread = P(("dp", "mp"), None)
    blocks = P("mp", None, None)
    table = P("mp", None)
    side = (blocks, blocks, table, blocks, table)
    return jax.shard_map(
        per_device,
        mesh=mesh,
        in_specs=(spread, P("dp"), blocks, table, blocks, table, spread)
        + (blocks, table, blocks, table) * 2,
        out_specs=(spread,) + side + side,
        check_vma=False,
    )
```

time: 82.4 us -> 71.2 us (0.86)
  Pallas kernels: 80.8 us -> 69.7 us
    pallas_call x2, Pallas kernels: 80.8 us -> 69.7 us  [the longest x1 66.7 us: exchange(): pl.pallas_call(exchange_kernel, out_shape=shapes, in_specs=[hbm] * 15, ou...]
where the time goes in v2:
time: 71.2 us; the launch traced here: 71 us
  Pallas kernels  69.7 us (98%)
  between operations  1.3 us (2%)
    pallas_call x1, Pallas kernels, exchange(): pl.pallas_call(exchange_kernel, out_shape=shapes, in_specs=[hbm] * 15, ou...  66.7 us
    pallas_call x1, Pallas kernels, exchange(): pl.pallas_call(deliver_kernel, out_shape=shapes, in_specs=[free] * 11, ou...  2.93 us

profile of v2, /device:TPU:1, one launch (start us, length us, event | category | flops | bytes accessed | tf_op | source)
XLA Modules:
  0.0 71.0 jit_solution(18346637524164307333)
XLA Ops:
  1.3 66.7 %exchange.1 = (bf16[1,8192]{1,0:T(2,128)(2,1)}, bf16[16,128,128]{2,1,0:T(8,128)(2,1)}, bf16[16,128,128]{2,1,0:T(8,128)(2,1)}, bf16[16,128,128]{2,1,0:T(8,128)(2,...) custom-call(bf16[1,8192]{1,0:T(2,128)(2,1)} %refs_0_.1, ...), custom_call_target="tpu_custom_call" | custom-call | flops 400000000 | bytes 8388608 | tf_op jit(solution)/shard_map/exchange/pallas_call | solution.py:563
  68.0 2.9 %deliver.1 = (bf16[1,8192]{1,0:T(2,128)(2,1)}, bf16[16,128,128]{2,1,0:T(8,128)(2,1)}, bf16[16,128,128]{2,1,0:T(8,128)(2,1)}, bf16[16,128,128]{2,1,0:T(8,128)(2,1...) custom-call(bf16[1,8192]{1,0:T(2,128)(2,1)} %get-tuple-element.33.re, ...), custom_call_target="tpu_custom_call" | custom-call | tf_op jit(solution)/shard_map/deliver/pallas_call | solution.py:641

commit v3 on v2

--- a/solution.py
+++ b/solution.py
@@ -66,30 +66,16 @@
         hub_in,
         hub_out,
         zrecv,
-        gbuf,
-        gscale,
-        relay,
-        rscale,
-        grecv,
-        gscale_in,
+        ypick,
+        yact,
         gsum,
         gsum_scale,
         w_sem,
         i_sem,
         o_sem,
-        zs_sem,
         zr_sem,
-        is_sem,
-        ir_sem,
-        ys_sem,
-        yr_sem,
-        ps_sem,
-        pr_sem,
-        cs_sem,
-        cr_sem,
-        fs_sem,
-        fr_sem,
-        gs_sem,
+        s_sem,
+        r_sem,
         gr_sem,
     ) = refs[26:]
     y = lax.axis_index("dp")
@@ -113,6 +99,12 @@
         return pltpu.make_async_remote_copy(
             src_ref=src, dst_ref=dst, send_sem=ssem, recv_sem=rsem, device_id=dev, device_id_type=MESH
         )
+
+    def arrived(part, sem):
+        remote(part, part, sem, sem, at_y(off(y, 1, NY))).wait_recv()
+
+    def left_here(part, sem):
+        remote(part, part, sem, sem, at_y(off(y, 1, NY))).wait_send()
 
     barrier = pltpu.get_barrier_semaphore()
     for d in Z_PEERS:
@@ -135,10 +127,10 @@
         )
     ]
     state_loads = [
-        [pltpu.make_async_copy(states_hbm[m][i], states_v.at[m, i], w_sem.at[5 + 3 * m + i]) for i in range(3)]
+        [pltpu.make_async_copy(states_hbm[m][i], states_v.at[m, i], w_sem.at[5 + 2 * m + (i > 0)]) for i in range(3)]
         for m in range(2)
     ]
-    scale_loads = [pltpu.make_async_copy(scales_hbm[i], scales_s.at[i], w_sem.at[11 + i]) for i in range(4)]
+    scale_loads = [pltpu.make_async_copy(scales_hbm[i], scales_s.at[i], w_sem.at[9]) for i in range(4)]
     for copy in loads:
         copy.start()
     state_loads[1][0].start()
@@ -170,7 +162,7 @@
 
     def z_copy(m, w, p, o):
         part = zbuf.at[w, pl.ds(m * COLS, COLS), :]
-        return remote(part, part, zs_sem.at[m, o], zr_sem.at[m, o], at_z(p))
+        return remote(part, part, s_sem.at[0], zr_sem.at[m, o // 4 if o % 4 == 0 else 0], at_z(p))
 
     def z_start(m, h, e):
         z_copy(m, off(z, -h, NZ), off(z, e, NZ), (-h - e) % NZ).start()
@@ -184,9 +176,9 @@
     for e in far:
         z_start(0, 0, e)
     for d in range(1, NS):
-        remote(idx_v.at[s], idx_v.at[s], is_sem.at[d], ir_sem.at[d], at_s(off(s, d, NS))).start()
+        remote(idx_v.at[s], idx_v.at[s], s_sem.at[1], r_sem.at[0], at_s(off(s, d, NS))).start()
     for d in range(1, NY):
-        remote(idx_y.at[0], idx_y.at[d], ys_sem.at[d], yr_sem.at[d], at_y(off(y, d, NY))).start()
+        remote(idx_y.at[0], idx_y.at[d], s_sem.at[2], r_sem.at[1], at_y(off(y, d, NY))).start()
     for e in near[0]:
         z_start(0, 0, e)
     for e in far:
@@ -196,14 +188,12 @@
         state_loads[m][2].start()
     for copy in scale_loads:
         copy.start()
-    for ref in (gscale, rscale, gsum_scale, scales_v):
+    for ref in (gsum_scale, scales_v):
         ref[...] = jnp.zeros_like(ref)
     for src in range(NS):
         rs_recv[src, K] = jnp.zeros((QROWS, BLK), BF16)
 
-    for d in range(1, NS):
-        p = off(s, -d, NS)
-        remote(idx_v.at[p], idx_v.at[p], is_sem.at[d], ir_sem.at[d], at_s(p)).wait_recv()
+    arrived(idx_v.at[pl.ds(0, NS - 1)], r_sem.at[0])
     to_smem = pltpu.make_async_copy(idx_v, idx_s, i_sem)
     to_smem.start()
 
@@ -223,9 +213,7 @@
     to_smem.wait()
 
     def pack_and_send(m):
-        for o in range(1, NZ):
-            if o % 4:
-                z_wait(m, o)
+        arrived(zbuf.at[pl.ds(0, 6)], zr_sem.at[m, 0])
         for w in range(NZ):
             flat[m, pl.ds(w, COLS, stride=NZ), :] = zbuf[w, m * COLS : (m + 1) * COLS, :].astype(F32)
 
@@ -233,7 +221,7 @@
             d = (s + i) % NS
             for k in range(K):
                 pack[m, i, k] = turned[m, idx_s[d, m, k]].astype(BF16)
-            remote(pack.at[m, i], picked.at[m, s], ps_sem.at[m, i], pr_sem.at[m, i], at_s(d)).start()
+            remote(pack.at[m, i], picked.at[m, s], s_sem.at[3], r_sem.at[2 + m], at_s(d)).start()
             return carry
 
         lax.fori_loop(1, NS, one, 0)
@@ -241,10 +229,19 @@
             picked[m, s, k] = turned[m, idx_s[s, m, k]].astype(BF16)
 
     def wait_picked(m):
-        for d in range(1, NS):
-            p = off(s, -d, NS)
-            remote(pack.at[m, d], picked.at[m, p], ps_sem.at[m, d], pr_sem.at[m, d], at_s(p)).wait_recv()
+        arrived(picked.at[m, pl.ds(0, NS - 1)], r_sem.at[2 + m])
         return jnp.concatenate([picked[m, :, k].reshape(ROWS, BLK) for k in range(K)], axis=1)
+
+    def y_copy(kind, d, p):
+        if kind < 2:
+            src, dst = picked.at[kind, :, pl.ds(p * 4, 4)], ypick.at[kind, d]
+        else:
+            src, dst = yact.at[kind - 2, 0], yact.at[kind - 2, d]
+        return remote(src, dst, s_sem.at[7 + kind // 2], r_sem.at[7 + kind], at_y(p))
+
+    def y_send(kind):
+        for d in range(1, NY):
+            y_copy(kind, d, off(y, d, NY)).start()
 
     pack_and_send(0)
     pack_and_send(1)
@@ -252,10 +249,13 @@
     state_loads[1][0].wait()
     state_loads[0][0].wait()
     a_in = wait_picked(0)
+    y_send(0)
     up_wide = jnp.concatenate([states_v[1, 0, k] for k in range(K)], axis=1)
     preact = lax.dot_general(a_in, up_wide, (((1,), (1,)), ((), ())), preferred_element_type=F32)
     squash = 1.0 / (1.0 + jnp.exp(-preact))
     hidden = (preact * squash).astype(BF16)
+    yact[0, 0] = hidden
+    y_send(2)
     down_tall = states_v[0, 0].reshape(K * BLK, BLK)
     contrib = lax.dot_general(hidden, down_tall, (((1,), (1,)), ((), ())), preferred_element_type=F32)
     for k in range(K):
@@ -263,7 +263,7 @@
     for d in range(1, NS):
         p = off(s, d, NS)
         remote(
-            cbuf.at[p], rs_recv.at[s, pl.ds(0, K)], cs_sem.at[d], cr_sem.at[d], at_s(p)
+            cbuf.at[p], rs_recv.at[s, pl.ds(0, K)], s_sem.at[4], r_sem.at[4], at_s(p)
         ).start()
     rs_recv[s, 0:K] = cbuf[s]
 
@@ -272,81 +272,47 @@
         code = jnp.round(grad * (CODE_TOP / jnp.maximum(top, 1e-30)))
         return code.astype(jnp.int32).astype(jnp.int16), top * (1.0 / CODE_TOP)
 
-    def grad_store(m, k, grad):
-        code, scale = coded(grad)
-        gbuf[m, k // 4, k // 2 % 2, k % 2] = code
-        gscale[m, k // 4, k // 2 % 2, k % 2 : k % 2 + 1, :] = scale
-
-    def pair(msg, m, buf, scl, at_src, to, to_scl, at_dst, p):
+    left, right, across = off(y, -1, NY), off(y, 1, NY), off(y, 2, NY)
+
+    def grad_msg(m, msg, at, p):
+        part, scales = gsum.at[at], gsum_scale.at[at]
         return (
-            remote(buf.at[at_src], to.at[at_dst], gs_sem.at[m, msg], gr_sem.at[m, msg], at_y(p)),
-            remote(scl.at[at_src], to_scl.at[at_dst], gs_sem.at[m, 10 + msg], gr_sem.at[m, 10 + msg], at_y(p)),
+            remote(part, part, s_sem.at[9], gr_sem.at[m, msg], at_y(p)),
+            remote(scales, scales, s_sem.at[10], gr_sem.at[m, 4 + msg], at_y(p)),
         )
 
-    left, right, across = off(y, -1, NY), off(y, 1, NY), off(y, 2, NY)
-
-    def grad_msg(m, msg):
-        raw, done = (m, gbuf, gscale), (m, gsum, gsum_scale)
-        if msg == 0:
-            return pair(msg, *raw, (m, across, 1), grecv, gscale_in, (m, 0), right)
-        if msg == 1:
-            return pair(msg, *raw, (m, across, 0), grecv, gscale_in, (m, 1), left)
-        if msg == 2:
-            return pair(msg, *raw, (m, right, 0), grecv, gscale_in, (m, 2), right)
-        if msg == 3:
-            return pair(msg, *raw, (m, left, 1), grecv, gscale_in, (m, 3), left)
-        if msg == 4:
-            return pair(msg, m, relay, rscale, (m, 1), grecv, gscale_in, (m, 4), right)
-        if msg == 5:
-            return pair(msg, m, relay, rscale, (m, 0), grecv, gscale_in, (m, 5), left)
-        if msg == 6:
-            return pair(msg, *done, (m, y), gsum, gsum_scale, (m, y), right)
-        if msg == 7:
-            return pair(msg, *done, (m, y), gsum, gsum_scale, (m, y), left)
-        if msg == 8:
-            return pair(msg, *done, (m, left, 1), gsum, gsum_scale, (m, left, 1), right)
-        return pair(msg, *done, (m, right, 0), gsum, gsum_scale, (m, right, 0), left)
+    def grad_out(m, msg):
+        at = ((m, y), (m, y), (m, left, 1), (m, right, 0))[msg]
+        return grad_msg(m, msg, at, (right, left)[msg % 2])
 
     def grad_send(m, *msgs):
         for msg in msgs:
-            for copy in grad_msg(m, msg):
+            for copy in grad_out(m, msg):
                 copy.start()
 
-    def grad_sent(m, *msgs):
-        for msg in msgs:
-            for copy in grad_msg(m, msg):
-                copy.wait_send()
-
-    def grad_wait(m, msg):
-        for copy in grad_msg(m, msg):
+    def grad_back(m, msg):
+        at = ((m, left), (m, right), (m, across, 1), (m, across, 0))[msg]
+        for copy in grad_msg(m, msg, at, left):
             copy.wait_recv()
 
-    def grad_back(m, msg, q):
-        at = (m, q) if msg < 8 else (m, q, 9 - msg)
-        for copy in pair(msg, m, gsum, gsum_scale, at, gsum, gsum_scale, at, left):
-            copy.wait_recv()
-
-    def value(buf, scl, at, b):
-        return buf[(*at, b)].astype(F32) * scl[(*at, slice(b, b + 1), slice(None))]
-
-    def pass_sum(m, msg, half, q, out):
-        grad_wait(m, msg)
-        for b in range(2):
-            code, scale = coded(value(grecv, gscale_in, (m, msg), b) + value(gbuf, gscale, (m, q, half), b))
-            relay[m, half, b] = code
-            rscale[m, half, b : b + 1, :] = scale
-        grad_send(m, out)
-
-    def own_sum(m, half, msgs):
-        for msg in msgs:
-            grad_wait(m, msg)
-        for b in range(2):
-            total = value(gbuf, gscale, (m, y, half), b)
-            for msg in msgs:
-                total = total + value(grecv, gscale_in, (m, msg), b)
-            code, scale = coded(total * per_token)
-            gsum[m, y, half, b] = code
-            gsum_scale[m, y, half, b : b + 1, :] = scale
+    def own_grad(m):
+        arrived(yact.at[m, pl.ds(0, NY - 1)], r_sem.at[9 + m])
+        arrived(ypick.at[1 - m, pl.ds(0, NY - 1)], r_sem.at[8 - m])
+        total = None
+        for d in range(NY):
+            if d:
+                wide = jnp.concatenate([ypick[1 - m, d, :, k].reshape(ROWS, BLK) for k in range(4)], axis=1)
+            else:
+                wide = jnp.concatenate([picked[1 - m, :, y * 4 + k].reshape(ROWS, BLK) for k in range(4)], axis=1)
+            narrow = yact[m, d]
+            pair = (narrow, wide) if m else (wide, narrow)
+            part = lax.dot_general(*pair, (((0,), (0,)), ((), ())), preferred_element_type=F32)
+            total = part if total is None else total + part
+        for k in range(4):
+            cut = slice(k * BLK, (k + 1) * BLK)
+            code, scale = coded((total[:, cut] if m else total[cut, :]) * per_token)
+            gsum[m, y, k // 2, k % 2] = code
+            gsum_scale[m, y, k // 2, k % 2 : k % 2 + 1, :] = scale
 
     lane = lax.broadcasted_iota(jnp.int32, (8, K), 1)
 
@@ -388,46 +354,25 @@
 
     def out_copy(m, q, i):
         rows = pl.ds(q * 4, 4)
-        return pltpu.make_async_copy(states_v.at[m, i, rows], new_hbm[m][i].at[rows], o_sem.at[m, i, q])
+        return pltpu.make_async_copy(states_v.at[m, i, rows], new_hbm[m][i].at[rows], o_sem)
 
     cot_in = wait_picked(1)
-    down_grad = lax.dot_general(cot_in, hidden, (((0,), (0,)), ((), ())), preferred_element_type=F32)
-    for k in range(K):
-        grad_store(0, k, down_grad[k * BLK : (k + 1) * BLK, :])
-
-    grad_send(0, 0, 1, 2, 3)
     hidden_grad = jnp.dot(cot_in, down_tall, preferred_element_type=F32)
-    pre_grad = (hidden_grad * squash * (1.0 + preact * (1.0 - squash))).astype(BF16)
-    up_grad = lax.dot_general(pre_grad, a_in, (((0,), (0,)), ((), ())), preferred_element_type=F32)
-    for k in range(K):
-        grad_store(1, k, up_grad[:, k * BLK : (k + 1) * BLK])
-    grad_send(1, 0, 1, 2, 3)
-
-    for m in range(2):
-        for o in range(1, NZ):
-            z_copy(m, z, off(z, 1, NZ), o).wait_send()
-        for d in range(1, NS):
-            remote(pack.at[m, d], picked.at[m, s], ps_sem.at[m, d], pr_sem.at[m, d], at_s(off(s, d, NS))).wait_send()
-    for d in range(1, NS):
-        remote(idx_v.at[s], idx_v.at[s], is_sem.at[d], ir_sem.at[d], at_s(off(s, d, NS))).wait_send()
-    for d in range(1, NY):
-        remote(idx_y.at[0], idx_y.at[d], ys_sem.at[d], yr_sem.at[d], at_y(off(y, d, NY))).wait_send()
-    for d in range(1, NY):
-        p = off(y, -d, NY)
-        remote(idx_y.at[0], idx_y.at[d], ys_sem.at[d], yr_sem.at[d], at_y(p)).wait_recv()
+    yact[1, 0] = (hidden_grad * squash * (1.0 + preact * (1.0 - squash))).astype(BF16)
+    y_send(3)
+    y_send(1)
+
+    left_here(zbuf.at[pl.ds(0, NZ - 1)], s_sem.at[0])
+    left_here(idx_v.at[pl.ds(0, NS - 1)], s_sem.at[1])
+    left_here(idx_y.at[pl.ds(0, NY - 1)], s_sem.at[2])
+    left_here(pack.at[:, pl.ds(1, NS - 1)], s_sem.at[3])
+    arrived(idx_y.at[pl.ds(0, NY - 1)], r_sem.at[1])
     count = idx_y[0, 3:4, :]
     for d in range(1, NY):
         count = count + idx_y[d, 3:4, :]
     per_token = 1.0 / count.astype(F32)
 
-    pass_sum(0, 0, 1, right, 4)
-    pass_sum(0, 1, 0, left, 5)
-
-    for d in range(1, NS):
-        p = off(s, -d, NS)
-        remote(
-            cbuf.at[p], rs_recv.at[p, pl.ds(0, K)], cs_sem.at[d], cr_sem.at[d], at_s(p)
-        ).wait_recv()
+    arrived(cbuf.at[pl.ds(0, NS - 1)], r_sem.at[4])
 
     def gather_rows(r, carry):
         total = rs_recv[0, idx_s[0, 2, r]].astype(F32)
@@ -442,25 +387,22 @@
 
     core = s % 2
     hubs = (off(z + 12 * core, 2, NZ), off(z, 1, NZ), off(z, -1, NZ))
-    hub_from = (off(z + 4 * core, -2, NZ), off(z, -1, NZ), off(z, 1, NZ))
 
     def hub_copy(j, p):
-        return remote(zsend.at[p % 4], hub_in.at[j], fs_sem.at[j], fr_sem.at[j], at_z(p))
+        return remote(zsend.at[p % 4], hub_in.at[j], s_sem.at[5], r_sem.at[5], at_z(p))
 
     def row_copy(j, p):
-        return remote(hub_out.at[p // 4], zrecv.at[j], fs_sem.at[4 + j], fr_sem.at[4 + j], at_z(p))
+        return remote(hub_out.at[p // 4], zrecv.at[j], s_sem.at[6], r_sem.at[6], at_z(p))
 
     for j in range(3):
         hub_copy(j, hubs[j]).start()
 
-    pass_sum(1, 0, 1, right, 4)
-    pass_sum(1, 1, 0, left, 5)
-    own_sum(0, 0, (2, 5))
-    own_sum(0, 1, (3, 4))
-    grad_send(0, 6, 7)
-
-    for j in range(3):
-        hub_copy(j, hub_from[j]).wait_recv()
+    own_grad(1)
+    grad_send(1, 0, 1)
+    own_grad(0)
+    grad_send(0, 0, 1)
+
+    arrived(hub_in, r_sem.at[5])
     for w in range(4):
         part = zsend[z % 4, w].astype(F32)
         for j in range(3):
@@ -469,29 +411,25 @@
     for j in (2, 1, 3):
         row_copy(j, off(z, 4 * j, NZ)).start()
 
-    own_sum(1, 0, (2, 5))
-    own_sum(1, 1, (3, 4))
-    grad_send(1, 6, 7)
     for m in range(2):
-        for i in (1, 2):
-            state_loads[m][i].wait()
-    for copy in scale_loads:
-        copy.wait()
+        both = states_v.at[m, pl.ds(1, 2)]
+        pltpu.make_async_copy(both, both, w_sem.at[6 + 2 * m]).wait()
+    pltpu.make_async_copy(scales_s, scales_s, w_sem.at[9]).wait()
+    adam(1, y)
+    grad_back(1, 0)
+    grad_send(1, 2)
+    grad_back(1, 1)
+    grad_send(1, 3)
     adam(0, y)
-    adam(1, y)
-    grad_back(0, 6, left)
-    grad_send(0, 8)
-    grad_back(0, 7, right)
-    grad_send(0, 9)
-
-    grad_back(1, 6, left)
-    grad_send(1, 8)
-    grad_back(1, 7, right)
-    grad_send(1, 9)
+    grad_back(0, 0)
+    grad_send(0, 2)
+    grad_back(0, 1)
+    grad_send(0, 3)
+    adam(1, left)
+    adam(1, right)
     adam(0, left)
     adam(0, right)
-    for j in (1, 2, 3):
-        row_copy(j, off(z, -4 * j, NZ)).wait_recv()
+    arrived(hub_out.at[pl.ds(0, 3)], r_sem.at[6])
     row = hub_out[z // 4].astype(F32)
     for j in (1, 2, 3):
         row = row + zrecv[j].astype(F32)
@@ -500,33 +438,23 @@
         layer_ref[0:1, i * BLK : (i + 1) * BLK] = row[i : i + 1, :].astype(BF16)
     layer_out = pltpu.make_async_copy(layer_ref, layer_hbm, w_sem.at[0])
     layer_out.start()
-    for j in range(3):
-        hub_copy(j, hubs[j]).wait_send()
-    for j in (1, 2, 3):
-        row_copy(j, off(z, 4 * j, NZ)).wait_send()
-    for d in range(1, NS):
-        p = off(s, d, NS)
-        remote(cbuf.at[p], rs_recv.at[s, pl.ds(0, K)], cs_sem.at[d], cr_sem.at[d], at_s(p)).wait_send()
-    for m in range(2):
-        grad_sent(m, 0, 1, 2, 3, 4, 5)
-    adam(1, left)
-    adam(1, right)
-    for m in range(2):
-        grad_back(m, 8, across)
-        grad_back(m, 9, across)
+    left_here(hub_in, s_sem.at[5])
+    left_here(hub_out.at[pl.ds(0, 3)], s_sem.at[6])
+    left_here(cbuf.at[pl.ds(0, NS - 1)], s_sem.at[4])
+    left_here(ypick.at[:, pl.ds(0, NY - 1)], s_sem.at[7])
+    left_here(yact.at[:, pl.ds(0, NY - 1)], s_sem.at[8])
+    for m in (1, 0):
+        grad_back(m, 2)
+        grad_back(m, 3)
         adam(m, across)
-    scale_out = [pltpu.make_async_copy(scales_v.at[i], new_scales_hbm[i], w_sem.at[1 + i]) for i in range(4)]
+    scale_out = [pltpu.make_async_copy(scales_v.at[i], new_scales_hbm[i], w_sem.at[1]) for i in range(4)]
     for copy in scale_out:
         copy.start()
-    for m in range(2):
-        grad_sent(m, 6, 7, 8, 9)
+    left_here(gsum.at[:, pl.ds(0, 3)], s_sem.at[9])
+    left_here(gsum_scale.at[:, pl.ds(0, 3)], s_sem.at[10])
     layer_out.wait()
-    for m in range(2):
-        for q in range(NY):
-            for i in range(3):
-                out_copy(m, q, i).wait()
-    for copy in scale_out:
-        copy.wait()
+    pltpu.make_async_copy(states_v, states_v, o_sem).wait()
+    pltpu.make_async_copy(scales_v, scales_v, w_sem.at[1]).wait()
 
 
 def deliver_kernel(*refs):
@@ -540,15 +468,15 @@
             parts.append((i, pl.ds(0, refs[i].shape[0])))
     loads = [pltpu.make_async_copy(refs[i].at[at], held[i].at[at], in_sem.at[j]) for j, (i, at) in enumerate(parts)]
     stores = [
-        pltpu.make_async_copy(held[i].at[at], refs[n + i].at[at], out_sem.at[j]) for j, (i, at) in enumerate(parts)
+        pltpu.make_async_copy(held[i].at[at], refs[n + i].at[at], out_sem.at[i]) for i, at in parts
     ]
     for load in loads:
         load.start()
     for load, store in zip(loads, stores):
         load.wait()
         store.start()
-    for store in stores:
-        store.wait()
+    for i in range(n):
+        pltpu.make_async_copy(held[i], refs[n + i], out_sem.at[i]).wait()
 
 
 def exchange(tokens, cotangent, counts, up_cols, down_rows, up, down):
@@ -590,31 +518,17 @@
             pltpu.VMEM((3, 4, COLS, BLK), BF16),
             pltpu.VMEM((4, COLS, BLK), BF16),
             pltpu.VMEM((4, COLS, BLK), BF16),
+            pltpu.VMEM((2, NY, NS, 4, QROWS, BLK), BF16),
+            pltpu.VMEM((2, NY, ROWS, BLK), BF16),
             pltpu.VMEM((2, NY, 2, 2, BLK, BLK), jnp.int16),
             pltpu.VMEM((2, NY, 2, 8, BLK), F32),
-            pltpu.VMEM((2, 2, 2, BLK, BLK), jnp.int16),
-            pltpu.VMEM((2, 2, 8, BLK), F32),
-            pltpu.VMEM((2, 6, 2, BLK, BLK), jnp.int16),
-            pltpu.VMEM((2, 6, 8, BLK), F32),
-            pltpu.VMEM((2, NY, 2, 2, BLK, BLK), jnp.int16),
-            pltpu.VMEM((2, NY, 2, 8, BLK), F32),
-            dma((15,)),
+            dma((10,)),
             dma,
-            dma((2, 3, NY)),
-            dma((2, NZ)),
-            dma((2, NZ)),
-            dma((NS,)),
-            dma((NS,)),
-            dma((NY,)),
-            dma((NY,)),
-            dma((2, NS)),
-            dma((2, NS)),
-            dma((NS,)),
-            dma((NS,)),
-            dma((8,)),
-            dma((8,)),
-            dma((2, 20)),
-            dma((2, 20)),
+            dma,
+            dma((2, 4)),
+            dma((11,)),
+            dma((11,)),
+            dma((2, 8)),
         ],
         compiler_params=pltpu.CompilerParams(
             collective_id=1, has_side_effects=True, vmem_limit_bytes=60 << 20
@@ -643,7 +557,7 @@
         out_shape=shapes,
         in_specs=[free] * 11,
         out_specs=(hbm,) * 11,
-        scratch_shapes=[pltpu.VMEM(a.shape, a.dtype) for a in shapes] + [dma((17,)), dma((17,))],
+        scratch_shapes=[pltpu.VMEM(a.shape, a.dtype) for a in shapes] + [dma((17,)), dma((11,))],
         compiler_params=pltpu.CompilerParams(vmem_limit_bytes=60 << 20),
         name="deliver",
     )(*results)

time: 71.2 us -> 70.6 us (level)
  no operation moved by 1% of the time
where the time goes in v3:
time: 70.6 us; the launch traced here: 70.5 us
  Pallas kernels  69.2 us (98%)
  between operations  1.3 us (2%)
    pallas_call x1, Pallas kernels, exchange(): pl.pallas_call(exchange_kernel, out_shape=shapes, in_specs=[hbm] * 15, ou...  66.3 us
    pallas_call x1, Pallas kernels, exchange(): pl.pallas_call(deliver_kernel, out_shape=shapes, in_specs=[free] * 11, ou...  2.88 us

profile of v3, /device:TPU:1, one launch (start us, length us, event | category | flops | bytes accessed | tf_op | source)
XLA Modules:
  0.0 70.5 jit_solution(9948375845118358134)
XLA Ops:
  1.3 66.3 %exchange.1 = (bf16[1,8192]{1,0:T(2,128)(2,1)}, bf16[16,128,128]{2,1,0:T(8,128)(2,1)}, bf16[16,128,128]{2,1,0:T(8,128)(2,1)}, bf16[16,128,128]{2,1,0:T(8,128)(2,...) custom-call(bf16[1,8192]{1,0:T(2,128)(2,1)} %refs_0_.1, ...), custom_call_target="tpu_custom_call" | custom-call | flops 400000000 | bytes 8388608 | tf_op jit(solution)/shard_map/exchange/pallas_call | solution.py:491
  67.6 2.9 %deliver.1 = (bf16[1,8192]{1,0:T(2,128)(2,1)}, bf16[16,128,128]{2,1,0:T(8,128)(2,1)}, bf16[16,128,128]{2,1,0:T(8,128)(2,1)}, bf16[16,128,128]{2,1,0:T(8,128)(2,1...) custom-call(bf16[1,8192]{1,0:T(2,128)(2,1)} %get-tuple-element.33.re, ...), custom_call_target="tpu_custom_call" | custom-call | tf_op jit(solution)/shard_map/deliver/pallas_call | solution.py:555

commit v4 on v3

--- a/solution.py
+++ b/solution.py
@@ -68,6 +68,12 @@
         zrecv,
         ypick,
         yact,
+        gbuf,
+        gscale,
+        relay,
+        rscale,
+        grecv,
+        gscale_in,
         gsum,
         gsum_scale,
         w_sem,
@@ -188,7 +194,7 @@
         state_loads[m][2].start()
     for copy in scale_loads:
         copy.start()
-    for ref in (gsum_scale, scales_v):
+    for ref in (gscale, rscale, gsum_scale, scales_v):
         ref[...] = jnp.zeros_like(ref)
     for src in range(NS):
         rs_recv[src, K] = jnp.zeros((QROWS, BLK), BF16)
@@ -233,11 +239,11 @@
         return jnp.concatenate([picked[m, :, k].reshape(ROWS, BLK) for k in range(K)], axis=1)
 
     def y_copy(kind, d, p):
-        if kind < 2:
-            src, dst = picked.at[kind, :, pl.ds(p * 4, 4)], ypick.at[kind, d]
+        if kind:
+            src, dst = yact.at[0], yact.at[d]
         else:
-            src, dst = yact.at[kind - 2, 0], yact.at[kind - 2, d]
-        return remote(src, dst, s_sem.at[7 + kind // 2], r_sem.at[7 + kind], at_y(p))
+            src, dst = picked.at[0, :, pl.ds(p * 4, 4)], ypick.at[d]
+        return remote(src, dst, s_sem.at[7 + kind], r_sem.at[7 + kind], at_y(p))
 
     def y_send(kind):
         for d in range(1, NY):
@@ -254,8 +260,6 @@
     preact = lax.dot_general(a_in, up_wide, (((1,), (1,)), ((), ())), preferred_element_type=F32)
     squash = 1.0 / (1.0 + jnp.exp(-preact))
     hidden = (preact * squash).astype(BF16)
-    yact[0, 0] = hidden
-    y_send(2)
     down_tall = states_v[0, 0].reshape(K * BLK, BLK)
     contrib = lax.dot_general(hidden, down_tall, (((1,), (1,)), ((), ())), preferred_element_type=F32)
     for k in range(K):
@@ -295,24 +299,65 @@
         for copy in grad_msg(m, msg, at, left):
             copy.wait_recv()
 
-    def own_grad(m):
-        arrived(yact.at[m, pl.ds(0, NY - 1)], r_sem.at[9 + m])
-        arrived(ypick.at[1 - m, pl.ds(0, NY - 1)], r_sem.at[8 - m])
+    def own_store(m, half, b, total):
+        code, scale = coded(total * per_token)
+        gsum[m, y, half, b] = code
+        gsum_scale[m, y, half, b : b + 1, :] = scale
+
+    def own_up():
+        arrived(yact.at[pl.ds(0, NY - 1)], r_sem.at[8])
+        arrived(ypick.at[pl.ds(0, NY - 1)], r_sem.at[7])
         total = None
         for d in range(NY):
             if d:
-                wide = jnp.concatenate([ypick[1 - m, d, :, k].reshape(ROWS, BLK) for k in range(4)], axis=1)
+                wide = jnp.concatenate([ypick[d, :, k].reshape(ROWS, BLK) for k in range(4)], axis=1)
             else:
-                wide = jnp.concatenate([picked[1 - m, :, y * 4 + k].reshape(ROWS, BLK) for k in range(4)], axis=1)
-            narrow = yact[m, d]
-            pair = (narrow, wide) if m else (wide, narrow)
-            part = lax.dot_general(*pair, (((0,), (0,)), ((), ())), preferred_element_type=F32)
+                wide = jnp.concatenate([picked[0, :, y * 4 + k].reshape(ROWS, BLK) for k in range(4)], axis=1)
+            part = lax.dot_general(yact[d], wide, (((0,), (0,)), ((), ())), preferred_element_type=F32)
             total = part if total is None else total + part
         for k in range(4):
-            cut = slice(k * BLK, (k + 1) * BLK)
-            code, scale = coded((total[:, cut] if m else total[cut, :]) * per_token)
-            gsum[m, y, k // 2, k % 2] = code
-            gsum_scale[m, y, k // 2, k % 2 : k % 2 + 1, :] = scale
+            own_store(1, k // 2, k % 2, total[:, k * BLK : (k + 1) * BLK])
+
+    def ring(msg):
+        if msg < 4:
+            at = ((across, 1), (across, 0), (right, 0), (left, 1))[msg]
+            src, scl = gbuf.at[at], gscale.at[at]
+        else:
+            src, scl = relay.at[5 - msg], rscale.at[5 - msg]
+        to = at_y((right, left)[msg % 2])
+        r = 11 if msg < 2 else 13
+        return (
+            remote(src, grecv.at[msg], s_sem.at[11], r_sem.at[r], to),
+            remote(scl, gscale_in.at[msg], s_sem.at[12], r_sem.at[r + 1], to),
+        )
+
+    def ring_send(*msgs):
+        for msg in msgs:
+            for copy in ring(msg):
+                copy.start()
+
+    def own_value(q, half, b):
+        return gbuf[q, half, b].astype(F32) * gscale[q, half, b : b + 1, :]
+
+    def came(msg, b):
+        return grecv[msg, b].astype(F32) * gscale_in[msg, b : b + 1, :]
+
+    def ring_pass():
+        arrived(grecv.at[pl.ds(0, 2)], r_sem.at[11])
+        arrived(gscale_in.at[pl.ds(0, 2)], r_sem.at[12])
+        for msg, q in ((0, right), (1, left)):
+            for b in range(2):
+                code, scale = coded(came(msg, b) + own_value(q, 1 - msg, b))
+                relay[1 - msg, b] = code
+                rscale[1 - msg, b : b + 1, :] = scale
+        ring_send(4, 5)
+
+    def own_down():
+        arrived(grecv.at[pl.ds(2, 4)], r_sem.at[13])
+        arrived(gscale_in.at[pl.ds(2, 4)], r_sem.at[14])
+        for half in range(2):
+            for b in range(2):
+                own_store(0, half, b, own_value(y, half, b) + came(2 + half, b) + came(5 - half, b))
 
     lane = lax.broadcasted_iota(jnp.int32, (8, K), 1)
 
@@ -357,10 +402,16 @@
         return pltpu.make_async_copy(states_v.at[m, i, rows], new_hbm[m][i].at[rows], o_sem)
 
     cot_in = wait_picked(1)
+    down_grad = lax.dot_general(cot_in, hidden, (((0,), (0,)), ((), ())), preferred_element_type=F32)
+    for k in range(K):
+        code, scale = coded(down_grad[k * BLK : (k + 1) * BLK, :])
+        gbuf[k // 4, k // 2 % 2, k % 2] = code
+        gscale[k // 4, k // 2 % 2, k % 2 : k % 2 + 1, :] = scale
+    ring_send(0, 1)
     hidden_grad = jnp.dot(cot_in, down_tall, preferred_element_type=F32)
-    yact[1, 0] = (hidden_grad * squash * (1.0 + preact * (1.0 - squash))).astype(BF16)
-    y_send(3)
+    yact[0] = (hidden_grad * squash * (1.0 + preact * (1.0 - squash))).astype(BF16)
     y_send(1)
+    ring_send(2, 3)
 
     left_here(zbuf.at[pl.ds(0, NZ - 1)], s_sem.at[0])
     left_here(idx_v.at[pl.ds(0, NS - 1)], s_sem.at[1])
@@ -372,6 +423,8 @@
         count = count + idx_y[d, 3:4, :]
     per_token = 1.0 / count.astype(F32)
 
+    ring_pass()
+
     arrived(cbuf.at[pl.ds(0, NS - 1)], r_sem.at[4])
 
     def gather_rows(r, carry):
@@ -397,9 +450,9 @@
     for j in range(3):
         hub_copy(j, hubs[j]).start()
 
-    own_grad(1)
+    own_up()
     grad_send(1, 0, 1)
-    own_grad(0)
+    own_down()
     grad_send(0, 0, 1)
 
     arrived(hub_in, r_sem.at[5])
@@ -441,8 +494,10 @@
     left_here(hub_in, s_sem.at[5])
     left_here(hub_out.at[pl.ds(0, 3)], s_sem.at[6])
     left_here(cbuf.at[pl.ds(0, NS - 1)], s_sem.at[4])
-    left_here(ypick.at[:, pl.ds(0, NY - 1)], s_sem.at[7])
-    left_here(yact.at[:, pl.ds(0, NY - 1)], s_sem.at[8])
+    left_here(ypick.at[pl.ds(0, NY - 1)], s_sem.at[7])
+    left_here(yact.at[pl.ds(0, NY - 1)], s_sem.at[8])
+    left_here(grecv, s_sem.at[11])
+    left_here(gscale_in, s_sem.at[12])
     for m in (1, 0):
         grad_back(m, 2)
         grad_back(m, 3)
@@ -518,16 +573,22 @@
             pltpu.VMEM((3, 4, COLS, BLK), BF16),
             pltpu.VMEM((4, COLS, BLK), BF16),
             pltpu.VMEM((4, COLS, BLK), BF16),
-            pltpu.VMEM((2, NY, NS, 4, QROWS, BLK), BF16),
-            pltpu.VMEM((2, NY, ROWS, BLK), BF16),
+            pltpu.VMEM((NY, NS, 4, QROWS, BLK), BF16),
+            pltpu.VMEM((NY, ROWS, BLK), BF16),
+            pltpu.VMEM((NY, 2, 2, BLK, BLK), jnp.int16),
+            pltpu.VMEM((NY, 2, 8, BLK), F32),
+            pltpu.VMEM((2, 2, BLK, BLK), jnp.int16),
+            pltpu.VMEM((2, 8, BLK), F32),
+            pltpu.VMEM((6, 2, BLK, BLK), jnp.int16),
+            pltpu.VMEM((6, 8, BLK), F32),
             pltpu.VMEM((2, NY, 2, 2, BLK, BLK), jnp.int16),
             pltpu.VMEM((2, NY, 2, 8, BLK), F32),
             dma((10,)),
             dma,
             dma,
             dma((2, 4)),
-            dma((11,)),
-            dma((11,)),
+            dma((13,)),
+            dma((15,)),
             dma((2, 8)),
         ],
         compiler_params=pltpu.CompilerParams(

time: 70.6 us -> 68.5 us (0.970)
  Pallas kernels: 69.2 us -> 66.8 us
    pallas_call x1, Pallas kernels: 66.3 us -> 63.9 us  [exchange(): pl.pallas_call(exchange_kernel, out_shape=shapes, in_specs=[hbm] * 15, ou...]
where the time goes in v4:
time: 68.5 us; the launch traced here: 68.1 us
  Pallas kernels  66.8 us (98%)
  between operations  1.3 us (2%)
    pallas_call x1, Pallas kernels, exchange(): pl.pallas_call(exchange_kernel, out_shape=shapes, in_specs=[hbm] * 15, ou...  63.9 us
    pallas_call x1, Pallas kernels, exchange(): pl.pallas_call(deliver_kernel, out_shape=shapes, in_specs=[free] * 11, ou...  2.88 us

profile of v4, /device:TPU:1, one launch (start us, length us, event | category | flops | bytes accessed | tf_op | source)
XLA Modules:
  0.0 68.1 jit_solution(1115761719329779017)
XLA Ops:
  1.3 63.9 %exchange.1 = (bf16[1,8192]{1,0:T(2,128)(2,1)}, bf16[16,128,128]{2,1,0:T(8,128)(2,1)}, bf16[16,128,128]{2,1,0:T(8,128)(2,1)}, bf16[16,128,128]{2,1,0:T(8,128)(2,...) custom-call(bf16[1,8192]{1,0:T(2,128)(2,1)} %refs_0_.1, ...), custom_call_target="tpu_custom_call" | custom-call | flops 400000000 | bytes 8388608 | tf_op jit(solution)/shard_map/exchange/pallas_call | solution.py:546
  65.2 2.9 %deliver.1 = (bf16[1,8192]{1,0:T(2,128)(2,1)}, bf16[16,128,128]{2,1,0:T(8,128)(2,1)}, bf16[16,128,128]{2,1,0:T(8,128)(2,1)}, bf16[16,128,128]{2,1,0:T(8,128)(2,1...) custom-call(bf16[1,8192]{1,0:T(2,128)(2,1)} %get-tuple-element.33.re, ...), custom_call_target="tpu_custom_call" | custom-call | tf_op jit(solution)/shard_map/deliver/pallas_call | solution.py:616

commit v5 on v4

--- a/solution.py
+++ b/solution.py
@@ -282,11 +282,11 @@
         part, scales = gsum.at[at], gsum_scale.at[at]
         return (
             remote(part, part, s_sem.at[9], gr_sem.at[m, msg], at_y(p)),
-            remote(scales, scales, s_sem.at[10], gr_sem.at[m, 4 + msg], at_y(p)),
+            remote(scales, scales, s_sem.at[10], gr_sem.at[m, 6 + msg], at_y(p)),
         )
 
     def grad_out(m, msg):
-        at = ((m, y), (m, y), (m, left, 1), (m, right, 0))[msg]
+        at = ((m, y, 1), (m, y, 0), (m, left, 1), (m, right, 0), (m, y, 0), (m, y, 1))[msg]
         return grad_msg(m, msg, at, (right, left)[msg % 2])
 
     def grad_send(m, *msgs):
@@ -295,7 +295,7 @@
                 copy.start()
 
     def grad_back(m, msg):
-        at = ((m, left), (m, right), (m, across, 1), (m, across, 0))[msg]
+        at = ((m, left, 1), (m, right, 0), (m, across, 1), (m, across, 0), (m, left, 0), (m, right, 1))[msg]
         for copy in grad_msg(m, msg, at, left):
             copy.wait_recv()
 
@@ -450,10 +450,16 @@
     for j in range(3):
         hub_copy(j, hubs[j]).start()
 
+    for m in range(2):
+        both = states_v.at[m, pl.ds(1, 2)]
+        pltpu.make_async_copy(both, both, w_sem.at[6 + 2 * m]).wait()
+    pltpu.make_async_copy(scales_s, scales_s, w_sem.at[9]).wait()
     own_up()
-    grad_send(1, 0, 1)
+    grad_send(1, 0, 1, 4, 5)
+    adam(1, y)
     own_down()
-    grad_send(0, 0, 1)
+    grad_send(0, 0, 1, 4, 5)
+    adam(0, y)
 
     arrived(hub_in, r_sem.at[5])
     for w in range(4):
@@ -464,24 +470,25 @@
     for j in (2, 1, 3):
         row_copy(j, off(z, 4 * j, NZ)).start()
 
-    for m in range(2):
-        both = states_v.at[m, pl.ds(1, 2)]
-        pltpu.make_async_copy(both, both, w_sem.at[6 + 2 * m]).wait()
-    pltpu.make_async_copy(scales_s, scales_s, w_sem.at[9]).wait()
-    adam(1, y)
     grad_back(1, 0)
     grad_send(1, 2)
     grad_back(1, 1)
     grad_send(1, 3)
-    adam(0, y)
+    grad_back(1, 4)
+    adam(1, left)
+    grad_back(1, 5)
+    adam(1, right)
     grad_back(0, 0)
     grad_send(0, 2)
     grad_back(0, 1)
     grad_send(0, 3)
-    adam(1, left)
-    adam(1, right)
+    grad_back(0, 4)
     adam(0, left)
+    grad_back(0, 5)
     adam(0, right)
+    grad_back(1, 2)
+    grad_back(1, 3)
+    adam(1, across)
     arrived(hub_out.at[pl.ds(0, 3)], r_sem.at[6])
     row = hub_out[z // 4].astype(F32)
     for j in (1, 2, 3):
@@ -498,10 +505,9 @@
     left_here(yact.at[pl.ds(0, NY - 1)], s_sem.at[8])
     left_here(grecv, s_sem.at[11])
     left_here(gscale_in, s_sem.at[12])
-    for m in (1, 0):
-        grad_back(m, 2)
-        grad_back(m, 3)
-        adam(m, across)
+    grad_back(0, 2)
+    grad_back(0, 3)
+    adam(0, across)
     scale_out = [pltpu.make_async_copy(scales_v.at[i], new_scales_hbm[i], w_sem.at[1]) for i in range(4)]
     for copy in scale_out:
         copy.start()
@@ -589,7 +595,7 @@
             dma((2, 4)),
             dma((13,)),
             dma((15,)),
-            dma((2, 8)),
+            dma((2, 12)),
         ],
         compiler_params=pltpu.CompilerParams(
             collective_id=1, has_side_effects=True, vmem_limit_bytes=60 << 20

time: 68.5 us -> 68 us (level)
  no operation moved by 1% of the time
where the time goes in v5:
time: 68 us; the launch traced here: 67.8 us
  Pallas kernels  66.5 us (98%)
  between operations  1.3 us (2%)
    pallas_call x1, Pallas kernels, exchange(): pl.pallas_call(exchange_kernel, out_shape=shapes, in_specs=[hbm] * 15, ou...  63.6 us
    pallas_call x1, Pallas kernels, exchange(): pl.pallas_call(deliver_kernel, out_shape=shapes, in_specs=[free] * 11, ou...  2.88 us

profile of v5, /device:TPU:1, one launch (start us, length us, event | category | flops | bytes accessed | tf_op | source)
XLA Modules:
  0.0 67.8 jit_solution(4810714765032605209)
XLA Ops:
  1.3 63.6 %exchange.1 = (bf16[1,8192]{1,0:T(2,128)(2,1)}, bf16[16,128,128]{2,1,0:T(8,128)(2,1)}, bf16[16,128,128]{2,1,0:T(8,128)(2,1)}, bf16[16,128,128]{2,1,0:T(8,128)(2,...) custom-call(bf16[1,8192]{1,0:T(2,128)(2,1)} %refs_0_.1, ...), custom_call_target="tpu_custom_call" | custom-call | flops 400000000 | bytes 8388608 | tf_op jit(solution)/shard_map/exchange/pallas_call | solution.py:552
  64.9 2.9 %deliver.1 = (bf16[1,8192]{1,0:T(2,128)(2,1)}, bf16[16,128,128]{2,1,0:T(8,128)(2,1)}, bf16[16,128,128]{2,1,0:T(8,128)(2,1)}, bf16[16,128,128]{2,1,0:T(8,128)(2,1...) custom-call(bf16[1,8192]{1,0:T(2,128)(2,1)} %get-tuple-element.33.re, ...), custom_call_target="tpu_custom_call" | custom-call | tf_op jit(solution)/shard_map/deliver/pallas_call | solution.py:622

commit v6 on v5

--- a/solution.py
+++ b/solution.py
@@ -223,7 +223,8 @@
         for w in range(NZ):
             flat[m, pl.ds(w, COLS, stride=NZ), :] = zbuf[w, m * COLS : (m + 1) * COLS, :].astype(F32)
 
-        def one(i, carry):
+        def one(turn, carry):
+            i = (turn + 1) % (NS - 1) + 1
             d = (s + i) % NS
             for k in range(K):
                 pack[m, i, k] = turned[m, idx_s[d, m, k]].astype(BF16)
@@ -264,7 +265,7 @@
     contrib = lax.dot_general(hidden, down_tall, (((1,), (1,)), ((), ())), preferred_element_type=F32)
     for k in range(K):
         cbuf[:, k] = contrib[:, k * BLK : (k + 1) * BLK].astype(BF16).reshape(NS, QROWS, BLK)
-    for d in range(1, NS):
+    for d in (4, 3, 5, 2, 6, 1, 7):
         p = off(s, d, NS)
         remote(
             cbuf.at[p], rs_recv.at[s, pl.ds(0, K)], s_sem.at[4], r_sem.at[4], at_s(p)

time: 68 us -> 67.6 us (level)
  the two profiles are of different devices: /device:TPU:1 before, /device:TPU:32 now
where the time goes in v6:
time: 67.6 us; the launch traced here: 67.4 us
  Pallas kernels  66.1 us (98%)
  between operations  1.3 us (2%)
    pallas_call x1, Pallas kernels, exchange(): pl.pallas_call(exchange_kernel, out_shape=shapes, in_specs=[hbm] * 15, ou...  63.2 us
    pallas_call x1, Pallas kernels, exchange(): pl.pallas_call(deliver_kernel, out_shape=shapes, in_specs=[free] * 11, ou...  2.88 us

profile of v6, /device:TPU:32, one launch (start us, length us, event | category | flops | bytes accessed | tf_op | source)
XLA Modules:
  0.0 67.4 jit_solution(16944193560251057568)
XLA Ops:
  1.3 63.2 %exchange.1 = (bf16[1,8192]{1,0:T(2,128)(2,1)}, bf16[16,128,128]{2,1,0:T(8,128)(2,1)}, bf16[16,128,128]{2,1,0:T(8,128)(2,1)}, bf16[16,128,128]{2,1,0:T(8,128)(2,...) custom-call(bf16[1,8192]{1,0:T(2,128)(2,1)} %refs_0_.1, ...), custom_call_target="tpu_custom_call" | custom-call | flops 400000000 | bytes 8388608 | tf_op jit(solution)/shard_map/exchange/pallas_call | solution.py:553
  64.5 2.9 %deliver.1 = (bf16[1,8192]{1,0:T(2,128)(2,1)}, bf16[16,128,128]{2,1,0:T(8,128)(2,1)}, bf16[16,128,128]{2,1,0:T(8,128)(2,1)}, bf16[16,128,128]{2,1,0:T(8,128)(2,1...) custom-call(bf16[1,8192]{1,0:T(2,128)(2,1)} %get-tuple-element.33.re, ...), custom_call_target="tpu_custom_call" | custom-call | tf_op jit(solution)/shard_map/deliver/pallas_call | solution.py:623
